TPU v7x, 128 devices: a whole 4x4x4 slice. The times are simulated.
128 devices in a mesh: along: 8 (over y, core), depth: 16 (over x, z).
Axes of the slice: x: 4, y: 4, z: 4, core: 2. Of those that a mesh axis runs over, the one named last changes fastest.
Arguments:
- right_side: float32 [3, 20, 8, 16, 1024], P(None, None, 'along', 'depth'), may hold values from -6 to 6
- shear_modulus: float32 [8, 16, 1024], P('along', 'depth'), may hold values from 0.5 to 2
- lame_lambda: float32 [8, 16, 1024], P('along', 'depth'), may hold values from 0.5 to 2
- stiff_shear: float32 [60, 60], replicated, may hold values from -0.1 to 1.8, as said below
- stiff_lame: float32 [60, 60], replicated, may hold values from -0.1 to 1.8, as said below
- face_interp: float32 [12, 4, 20], replicated, may hold values from -0.875 to 0.875
- neighbours: int32 [8, 16, 4096], P('along', 'depth'), may hold values from 0 to 4607, as said below
- fault_count: int32 [8, 16], P('along', 'depth'), may hold values from 0 to 2048, as said below
- fault_owner: int32 [8, 16, 2048], P('along', 'depth'), may hold values from 0 to 127, as said below
- fault_slot: int32 [8, 16, 2048], P('along', 'depth'), may hold values from 0 to 511, as said below
- fault_face: int32 [8, 16, 2048], P('along', 'depth'), may hold values from 0 to 4095, as said below
- normal_stress: float32 [12, 65536], P(None, ('along', 'depth')), may hold values from 1 to 10
- friction: float32 [12, 65536], P(None, ('along', 'depth')), may hold values from 0.3 to 1
- state_factor: float32 [12, 65536], P(None, ('along', 'depth')), may hold values from 0.5 to 8
- shear_load: float32 [2, 12, 65536], P(None, None, ('along', 'depth')), may hold values from -6 to 6
Outputs:
- displacement: float32 [3, 20, 8, 16, 1024], P(None, None, 'along', 'depth')
- residual: float32 [3, 20, 8, 16, 1024], P(None, None, 'along', 'depth')
- slip_rate: float32 [12, 65536], P(None, ('along', 'depth'))
Inputs may be any that keep to these rules, and one draw needn't show every extreme that they name: `neighbours`: slots below 4096 other than 3072 + e for e < 512 are paired: each names its partner and its partner names it; slot 3072 + e for e < 512 names 4096 + e. `fault_count`: the counts of all partitions add up to 65536. `fault_owner`: owners are flat device indices along * 16 + depth; entries at or past a partition's count are zero. Every grid point of every owner is named by exactly one live fault face; among the live faces of one partition no owner is named more than 16 times, and in every draw some partition names every owner exactly 16 times. `fault_slot`: entries at or past a partition's count are zero. `fault_face`: the slots of one partition are distinct. `stiff_shear`: Symmetric. `stiff_lame`: Symmetric.
All inputs are finite; a program needn't handle non-finite values.
Results may differ from a plain program's by a relative error of at most 0.0003.
Values sent between devices are 32-bit elements; how exact they have to be, the bound alone decides.
A program may use at most 128 MiB of HBM per device.

v0:
```python
import jax
import jax.numpy as jnp
from jax import lax
from jax.sharding import PartitionSpec as P

ITERS = 4
NEWTON = 6


highest = lax.Precision.HIGHEST
damping = 0.5
time_step = 0.5
lower_edge = 0.25
upper_edge = 5.0


def padded(block, sides, width):
    for axis, dim in sides:
        count = lax.axis_size(axis)
        forward = [(i, i + 1) for i in range(count - 1)]
        backward = [(target, source) for source, target in forward]
        low = lax.ppermute(
            lax.slice_in_dim(block, block.shape[dim] - width, None, axis=dim), axis, forward
        )
        high = lax.ppermute(lax.slice_in_dim(block, 0, width, axis=dim), axis, backward)
        block = jnp.concatenate([low, block, high], axis=dim)
    return block


def inverse_sinh(value):
    size_abs = jnp.abs(value)
    sign_of = jnp.where(value < 0.0, -1.0, 1.0)
    return sign_of * jnp.log(size_abs + jnp.sqrt(size_abs * size_abs + 1.0))


def slip_law(traction, normal_stress, friction, state_factor, shear_load):
    effective = normal_stress * (1.0 + 0.5 * jnp.tanh(traction[2]))
    strike = shear_load[0] + traction[0]
    updip = shear_load[1] + traction[1]
    magnitude = jnp.sqrt(strike * strike + updip * updip)
    resist = friction * effective
    velocity = jnp.zeros_like(magnitude)
    for sweep in range(NEWTON):
        scaled = state_factor * velocity
        misfit = magnitude - damping * velocity - resist * inverse_sinh(scaled)
        slope = -damping - resist * state_factor / jnp.sqrt(1.0 + scaled * scaled)
        velocity = velocity - misfit / slope
    factor = time_step * velocity / jnp.maximum(magnitude, 1.0)
    return (velocity, jnp.stack([factor * strike, factor * updip]))


def face_flux(field, material, links, face_interp):
    qpts = face_interp.shape[0]
    elems = field.shape[-1]
    side = elems // 8
    traces = jnp.einsum("qfn,cne->cqfe", face_interp, field, precision=highest).reshape(
        3, qpts, 4 * elems
    )
    rims = traces[:, :, 3 * elems : 3 * elems + 4 * side].reshape(3 * qpts, 4, side)
    rim_material = material[: 4 * side].reshape(1, 4, side)
    packed = jnp.concatenate([rims, rim_material], axis=0).transpose(1, 0, 2)
    along_ext = padded(packed[0:2], (("along", 0),), 1)
    depth_ext = padded(packed[2:4], (("depth", 0),), 1)
    arrived = jnp.stack([along_ext[0], along_ext[3], depth_ext[0], depth_ext[3]], axis=0)
    arrived_traces = arrived[:, : 3 * qpts].transpose(1, 0, 2).reshape(3, qpts, 4 * side)
    arrived_material = arrived[:, 3 * qpts].reshape(4 * side)
    own_material = jnp.concatenate([material] * 4)
    table = jnp.concatenate([traces, arrived_traces], axis=-1)
    material_table = jnp.concatenate([own_material, arrived_material])
    other = table[:, :, links]
    other_material = material_table[links]
    return 0.5 * (own_material + other_material) * (traces - other)


def on_device(
    right_side,
    shear_modulus,
    lame_lambda,
    stiff_shear,
    stiff_lame,
    face_interp,
    neighbours,
    fault_count,
    fault_owner,
    fault_slot,
    fault_face,
    normal_stress,
    friction,
    state_factor,
    shear_load,
):
    elems = right_side.shape[-1]
    qpts = face_interp.shape[0]
    nodes = right_side.shape[1]
    fmax = fault_owner.shape[-1]
    face_own = normal_stress.shape[-1]
    load = right_side.reshape(3, nodes, elems)
    shear = shear_modulus.reshape(elems)
    lame = lame_lambda.reshape(elems)
    material = lame + 2.0 * shear
    links = neighbours.reshape(4 * elems)
    faces = fault_face.reshape(fmax)
    stacked = jnp.concatenate([stiff_shear, stiff_lame], axis=0)
    width = 3 * nodes
    devices = lax.axis_size(("along", "depth"))
    cap = fmax // devices
    slots_all = devices * cap
    count = fault_count.reshape(())
    owner = fault_owner.reshape(fmax)
    slot = fault_slot.reshape(fmax)
    order = jnp.arange(fmax)
    live = order < count
    onehot = ((owner[:, None] == jnp.arange(devices)[None, :]) & live[:, None]).astype(jnp.int32)
    earlier = jnp.cumsum(onehot, axis=0) - onehot
    ranking = jnp.sum(earlier * onehot, axis=1)
    place = jnp.where(live, owner * cap + ranking, slots_all)
    pick = jnp.minimum(place, slots_all - 1)
    send_ids = jnp.full((1, slots_all), -1, jnp.int32).at[0, place].set(slot, mode="drop")
    center = 0.5 * (upper_edge + lower_edge)
    spread = 0.5 * (upper_edge - lower_edge)
    ratio = center / spread
    rho = 1.0 / ratio
    solution = jnp.zeros_like(load)
    residual = load
    direction = residual / (center * material)
    for sweep in range(ITERS):
        solution = solution + direction
        flux = face_flux(direction, material, links, face_interp)
        lifted = jnp.einsum(
            "qfn,cqfe->cne", face_interp, flux.reshape(3, qpts, 4, elems), precision=highest
        )
        product = jnp.dot(stacked, direction.reshape(width, elems), precision=highest)
        volume = shear * product[:width] + lame * product[width:]
        image, flux = (volume.reshape(3, nodes, elems) + lifted, flux)
        residual = residual - image
        rho_next = 1.0 / (2.0 * ratio - rho)
        direction = rho_next * rho * direction + 2.0 * rho_next / spread * residual / material
        rho = rho_next
    traction = face_flux(solution, material, links, face_interp)[:, :, faces]
    live_float = live.astype(jnp.float32)[None, None, :]
    send_traction = (
        jnp.zeros((3 * qpts, slots_all), jnp.float32)
        .at[:, place]
        .set(traction.reshape(3 * qpts, fmax), mode="drop")
    )
    got_traction, got_ids = (
        lax.all_to_all(send_traction, ("along", "depth"), split_axis=1, concat_axis=1, tiled=True),
        lax.all_to_all(send_ids, ("along", "depth"), split_axis=1, concat_axis=1, tiled=True),
    )
    valid = got_ids[0] >= 0
    index = jnp.where(valid, got_ids[0], 0)
    rate, slip = slip_law(
        got_traction.reshape(3, qpts, slots_all),
        normal_stress[:, index],
        friction[:, index],
        state_factor[:, index],
        shear_load[:, :, index],
    )
    slip_rate = (
        jnp.zeros((qpts, face_own), jnp.float32)
        .at[:, jnp.where(valid, index, face_own)]
        .set(rate, mode="drop")
    )
    outgoing = slip.reshape(2 * qpts, slots_all)
    back = lax.all_to_all(outgoing, ("along", "depth"), split_axis=1, concat_axis=1, tiled=True)
    returned = back[:, pick].reshape(2, qpts, fmax) * live_float
    face_kind = faces // elems
    element = faces % elems
    interp = face_interp[:, face_kind, :]
    values = 0.5 * jnp.einsum("qjn,cqj->cnj", interp, returned, precision=highest)
    jump = jnp.zeros((2, nodes, elems), jnp.float32).at[:, :, element].add(values)
    displacement = solution + jnp.concatenate(
        [jump, jnp.zeros((1, nodes, elems), jnp.float32)], axis=0
    )
    return (displacement.reshape(right_side.shape), residual.reshape(right_side.shape), slip_rate)


def solution(mesh):
    in_specs = (
        P(None, None, "along", "depth", None),
        P("along", "depth", None),
        P("along", "depth", None),
        P(),
        P(),
        P(),
        P("along", "depth", None),
        P("along", "depth"),
        P("along", "depth", None),
        P("along", "depth", None),
        P("along", "depth", None),
        P(None, ("along", "depth")),
        P(None, ("along", "depth")),
        P(None, ("along", "depth")),
        P(None, None, ("along", "depth")),
    )
    out_specs = (
        P(None, None, "along", "depth", None),
        P(None, None, "along", "depth", None),
        P(None, ("along", "depth")),
    )
    return jax.shard_map(
        on_device, mesh=mesh, in_specs=in_specs, out_specs=out_specs, check_vma=False
    )
```

profile of v0, /device:TPU:1, one launch (start us, length us, event | category | flops | bytes accessed | tf_op | source)
XLA Modules:
  0.0 755.7 jit_solution(17184441367016557342)
XLA Ops:
  20.4 8.2 %scatter_custom_fusion.3 = s32[2048]{0:T(1024)S(1)} fusion(s32[2048]{0:T(1024)S(1)} %broadcast_select_fusion, s32[2048]{0:T(1024)} %bitcast.444, s32[]{:T(128)} %constant.22.clone.1), kind=kCustom, calls=%fused_computation.271 | custom fusion | bytes 8704
  29.4 13.1 %all-to-all-start = ((s32[1,128,16]{2,0,1:T(1,128)}), s32[1,128,16]{2,0,1:T(1,128)S(1)}, u32[]{:S(2)}, u32[]{:S(2)}) async-start(s32[1,128,16]{2,0,1:T(1,128)} %bitcast.57), calls=%async_computation | async-start | bytes 131072 | tf_op jit(solution)/shard_map/all_to_all | solution.py:148
  48.1 37.4 %gather_fusion.14 = f32[2048,12,20]{2,0,1:T(8,128)} fusion(f32[12,4,20]{2,1,0:T(4,128)S(1)} %copy-done, s32[2048]{0:T(1024)S(1)} %get-tuple-element.72), kind=kCustom, calls=%fused_computation.14 | custom fusion | bytes 3940352 | tf_op jit(solution)/shard_map/gather | solution.py:169
  107.4 15.6 %gather_fusion.6 = f32[2048,2,12]{2,1,0:T(2,128)} fusion(f32[2,12,512]{1,0,2:T(2,128)} %copy.368, s32[2048]{0:T(1024)S(1)} %get-tuple-element.75), kind=kCustom, calls=%fused_computation.6 | custom fusion | bytes 401408 | tf_op jit(solution)/shard_map/gather | solution.py:157
  125.7 23.0 %gather_fusion = f32[4096]{0:T(1024)S(1)} fusion(f32[4608]{0:T(1024)S(1)} %constant_dynamic-update-slice_fusion, s32[4096]{0:T(1024)S(1)} %broadcast_clamp_fusion), kind=kCustom, calls=%fused_computation | custom fusion | bytes 49152 | tf_op jit(solution)/shard_map/gather | solution.py:71
  149.9 7.6 %copy.349 = f32[3,12,4608]{1,0,2:T(4,128)} copy(f32[3,12,4608]{2,1,0:T(8,128)} %pad_maximum_fusion) | data formatting | bytes 1327104 | tf_op jit(solution)/shard_map/concatenate | solution.py:68
  157.5 34.0 %gather_fusion.1 = f32[4096,3,12]{2,1,0:T(4,128)} fusion(f32[3,12,4608]{1,0,2:T(4,128)} %copy.349, s32[4096]{0:T(1024)S(1)} %broadcast_clamp_fusion), kind=kCustom, calls=%fused_computation.1 | custom fusion | bytes 1196032 | tf_op jit(solution)/shard_map/gather | solution.py:70
  191.5 6.5 copy.351
  218.3 23.0 %gather_fusion.2 = f32[4096]{0:T(1024)S(1)} fusion(f32[4608]{0:T(1024)S(1)} %constant_dynamic-update-slice_fusion.1, s32[4096]{0:T(1024)S(1)} %broadcast_clamp_fusion), kind=kCustom, calls=%fused_computation.2 | custom fusion | bytes 49152 | tf_op jit(solution)/shard_map/gather | solution.py:71
  242.5 7.6 %copy.355 = f32[3,12,4608]{1,0,2:T(4,128)} copy(f32[3,12,4608]{2,1,0:T(8,128)} %pad_maximum_fusion.1) | data formatting | bytes 1327104 | tf_op jit(solution)/shard_map/concatenate | solution.py:68
  250.1 34.0 %gather_fusion.3 = f32[4096,3,12]{2,1,0:T(4,128)} fusion(f32[3,12,4608]{1,0,2:T(4,128)} %copy.355, s32[4096]{0:T(1024)S(1)} %broadcast_clamp_fusion), kind=kCustom, calls=%fused_computation.3 | custom fusion | bytes 1196032 | tf_op jit(solution)/shard_map/gather | solution.py:70
  284.1 6.5 copy.357
  310.9 23.0 %gather_fusion.4 = f32[4096]{0:T(1024)S(1)} fusion(f32[4608]{0:T(1024)S(1)} %constant_dynamic-update-slice_fusion.2, s32[4096]{0:T(1024)S(1)} %broadcast_clamp_fusion), kind=kCustom, calls=%fused_computation.4 | custom fusion | bytes 49152 | tf_op jit(solution)/shard_map/gather | solution.py:71
  335.1 7.6 %copy.361 = f32[3,12,4608]{1,0,2:T(4,128)} copy(f32[3,12,4608]{2,1,0:T(8,128)} %pad_maximum_fusion.2) | data formatting | bytes 1327104 | tf_op jit(solution)/shard_map/concatenate | solution.py:68
  342.6 34.0 %gather_fusion.5 = f32[4096,3,12]{2,1,0:T(4,128)} fusion(f32[3,12,4608]{1,0,2:T(4,128)} %copy.361, s32[4096]{0:T(1024)S(1)} %broadcast_clamp_fusion), kind=kCustom, calls=%fused_computation.5 | custom fusion | bytes 1196032 | tf_op jit(solution)/shard_map/gather | solution.py:70
  376.6 6.5 copy.363
  420.2 23.0 %gather_fusion.15 = f32[4096]{0:T(1024)S(1)} fusion(f32[4608]{0:T(1024)S(1)} %constant_dynamic-update-slice_fusion.4, s32[4096]{0:T(1024)S(1)} %broadcast_clamp_fusion), kind=kCustom, calls=%fused_computation.15 | custom fusion | bytes 49152 | tf_op jit(solution)/shard_map/gather | solution.py:71
  443.4 23.0 %gather_fusion.7 = f32[4096]{0:T(1024)S(1)} fusion(f32[4608]{0:T(1024)S(1)} %constant_dynamic-update-slice_fusion.3, s32[4096]{0:T(1024)S(1)} %broadcast_clamp_fusion), kind=kCustom, calls=%fused_computation.7 | custom fusion | bytes 49152 | tf_op jit(solution)/shard_map/gather | solution.py:71
  466.6 6.3 copy.372
  472.9 34.0 %gather_fusion.8 = f32[4096,3,12]{2,1,0:T(4,128)} fusion(f32[3,12,4608]{1,0,2:T(4,128)} %copy.372, s32[4096]{0:T(1024)S(1)} %broadcast_clamp_fusion), kind=kCustom, calls=%fused_computation.8 | custom fusion | bytes 1196032 | tf_op jit(solution)/shard_map/gather | solution.py:70
  506.9 6.5 copy.373
  513.5 5.9 copy.374
  519.5 18.8 %gather_fusion.9 = f32[2048,3,12]{2,1,0:T(4,128)} fusion(f32[3,12,4096]{1,0,2:T(4,128)} %copy.374, s32[2048]{0:T(1024)S(1)} %copy-done.19), kind=kCustom, calls=%fused_computation.9 | custom fusion | bytes 598016 | tf_op jit(solution)/shard_map/gather | solution.py:139
  543.1 6.2 scatter_custom_fusion
  551.1 17.1 %all-to-all-start.1 = ((f32[128,1,576]{2,1,0:T(1,128)}), f32[128,1,576]{2,1,0:T(1,128)S(1)}, u32[]{:S(2)}, u32[]{:S(2)}) async-start(f32[128,1,576]{2,1,0:T(1,128)} %reshape.959), calls=%async_computation.1 | async-start | bytes 655360 | tf_op jit(solution)/shard_map/all_to_all | solution.py:147
  568.2 7.6 %copy.393 = f32[3,12,4608]{1,0,2:T(4,128)} copy(f32[3,12,4608]{2,1,0:T(8,128)} %pad_maximum_fusion.4) | data formatting | bytes 1327104 | tf_op jit(solution)/shard_map/concatenate | solution.py:68
  575.8 34.0 %gather_fusion.16 = f32[4096,3,12]{2,1,0:T(4,128)} fusion(f32[3,12,4608]{1,0,2:T(4,128)} %copy.393, s32[4096]{0:T(1024)S(1)} %broadcast_clamp_fusion), kind=kCustom, calls=%fused_computation.16 | custom fusion | bytes 1196032 | tf_op jit(solution)/shard_map/gather | solution.py:70
  609.8 6.5 copy.395
  633.0 9.8 %all-to-all-start.2 = ((f32[128,1,384]{2,1,0:T(1,128)}), f32[128,1,384]{2,1,0:T(1,128)S(1)}, u32[]{:S(2)}, u32[]{:S(2)}) async-start(f32[128,1,384]{2,1,0:T(1,128)} %reshape.961), calls=%async_computation.2 | async-start | bytes 393216 | tf_op jit(solution)/shard_map/all_to_all | solution.py:165
  645.1 6.0 scatter_custom_fusion.2
  663.2 25.5 %fusion.11 = f32[2048,2,20]{2,1,0:T(2,128)S(1)} fusion(f32[2,12,2048]{1,0,2:T(2,128)} %copy.388, f32[12,2048,20]{2,1,0:T(8,128)} %bitcast.390), kind=kOutput, calls=%fused_computation.41 | convolution fusion | flops 11878400 | bytes 2490368 | tf_op jit(solution)/shard_map/qjn,cqj->cnj/dot_general | solution.py:170
  689.0 65.1 %scatter_fusion = f32[2,20,1024]{1,0,2:T(2,128)S(1)} fusion(f32[2,20,1024]{1,0,2:T(2,128)S(1)} %broadcast_in_dim.30, s32[2048]{0:T(1024)S(1)} %bitcast.437, f32[2048,2,20]{2,1,0:T(2,128)S(1)} %fusion.11), kind=kCustom, calls=%fused_computation.18 | custom fusion | flops 81920 | bytes 991232 | tf_op jit(solution)/shard_map/scatter-add | solution.py:171
  (267 shorter events, 169.7 us)
Async XLA Ops:
  0.7 47.4 %copy-start = (f32[12,4,20]{2,1,0:T(4,128)S(1)}, f32[12,4,20]{2,1,0:T(4,128)}, u32[]{:S(2)}) copy-start(f32[12,4,20]{2,1,0:T(4,128)} %param.20) | copy-start | bytes 11524
  0.8 45.0 %copy-start.20 = (f32[12,512]{1,0:T(8,128)S(1)}, f32[12,512]{1,0:T(8,128)}, u32[]{:S(2)}) copy-start(f32[12,512]{1,0:T(8,128)} %param.26) | copy-start | bytes 73732
  0.8 45.2 %copy-start.21 = (f32[12,512]{1,0:T(8,128)S(1)}, f32[12,512]{1,0:T(8,128)}, u32[]{:S(2)}) copy-start(f32[12,512]{1,0:T(8,128)} %param.27) | copy-start | bytes 73732
  0.8 45.3 %copy-start.22 = (f32[12,512]{1,0:T(8,128)S(1)}, f32[12,512]{1,0:T(8,128)}, u32[]{:S(2)}) copy-start(f32[12,512]{1,0:T(8,128)} %param.28) | copy-start | bytes 73732
  0.8 46.2 %copy-start.15 = (f32[2,12,512]{2,0,1:T(2,128)S(1)}, f32[2,12,512]{2,0,1:T(2,128)}, u32[]{:S(2)}) copy-start(f32[2,12,512]{2,0,1:T(2,128)} %param.29) | copy-start | bytes 147460
  4.4 121.3 %collective-permute-start = (f32[1,37,128]{2,0,1:T(1,128)S(1)}, f32[1,37,128]{2,0,1:T(1,128)S(1)}, u32[]{:S(2)}, u32[]{:S(2)}) collective-permute-start(f32[1,37,128]{2,0,1:T(1,128)S(1)} %get-tuple-element.58), channel_id=1, source_target_pairs={{0,16},{16,32},{32,48},{48,64},{64,80},{80,96},{96,112},{1,17},{17... | collective-permute-start | bytes 56840 | tf_op jit(solution)/shard_map/ppermute | solution.py:22
  9.0 116.7 %collective-permute-start.3 = (f32[1,37,128]{2,0,1:T(1,128)S(1)}, f32[1,37,128]{2,0,1:T(1,128)S(1)}, u32[]{:S(2)}, u32[]{:S(2)}) collective-permute-start(f32[1,37,128]{2,0,1:T(1,128)S(1)} %get-tuple-element.59), channel_id=1, source_target_pairs={{1,0},{2,1},{3,2},{4,3},{5,4},{6,5},{7,6},{8,7},{9,8},{10,9},{11,1... | collective-permute-start | bytes 56840 | tf_op jit(solution)/shard_map/ppermute | solution.py:25
  10.3 115.4 %collective-permute-start.2 = (f32[1,37,128]{2,0,1:T(1,128)S(1)}, f32[1,37,128]{2,0,1:T(1,128)S(1)}, u32[]{:S(2)}, u32[]{:S(2)}) collective-permute-start(f32[1,37,128]{2,0,1:T(1,128)S(1)} %get-tuple-element.60), channel_id=1, source_target_pairs={{0,1},{1,2},{2,3},{3,4},{4,5},{5,6},{6,7},{7,8},{8,9},{9,10},{10,1... | collective-permute-start | bytes 56840 | tf_op jit(solution)/shard_map/ppermute | solution.py:22
  14.5 111.2 %collective-permute-start.1 = (f32[1,37,128]{2,0,1:T(1,128)S(1)}, f32[1,37,128]{2,0,1:T(1,128)S(1)}, u32[]{:S(2)}, u32[]{:S(2)}) collective-permute-start(f32[1,37,128]{2,0,1:T(1,128)S(1)} %get-tuple-element.61), channel_id=1, source_target_pairs={{16,0},{32,16},{48,32},{64,48},{80,64},{96,80},{112,96},{17,1},{33... | collective-permute-start | bytes 56840 | tf_op jit(solution)/shard_map/ppermute | solution.py:25
  29.4 56.1 %all-to-all-start = ((s32[1,128,16]{2,0,1:T(1,128)}), s32[1,128,16]{2,0,1:T(1,128)S(1)}, u32[]{:S(2)}, u32[]{:S(2)}) async-start(s32[1,128,16]{2,0,1:T(1,128)} %bitcast.57), calls=%async_computation | async-start | bytes 131072 | tf_op jit(solution)/shard_map/all_to_all | solution.py:148
  149.9 48.2 %copy-start.6 = (f32[3,20,1024]{2,1,0:T(8,128)S(1)}, f32[3,20,1024]{2,1,0:T(8,128)}, u32[]{:S(2)}) copy-start(f32[3,20,1024]{2,1,0:T(8,128)} %reshape.716) | copy-start | bytes 737284
  204.4 12.7 %collective-permute-start.4 = (f32[1,37,128]{2,0,1:T(1,128)}, f32[1,37,128]{2,0,1:T(1,128)S(1)}, u32[]{:S(2)}, u32[]{:S(2)}) collective-permute-start(f32[1,37,128]{2,0,1:T(1,128)} %get-tuple-element.54), channel_id=1, source_target_pairs={{0,16},{16,32},{32,48},{48,64},{64,80},{80,96},{96,112},{1,17},{17... | collective-permute-start | bytes 56840 | tf_op jit(solution)/shard_map/ppermute | solution.py:22
  207.9 9.2 %collective-permute-start.7 = (f32[1,37,128]{2,0,1:T(1,128)}, f32[1,37,128]{2,0,1:T(1,128)S(1)}, u32[]{:S(2)}, u32[]{:S(2)}) collective-permute-start(f32[1,37,128]{2,0,1:T(1,128)} %get-tuple-element.55), channel_id=1, source_target_pairs={{1,0},{2,1},{3,2},{4,3},{5,4},{6,5},{7,6},{8,7},{9,8},{10,9},{11,1... | collective-permute-start | bytes 56840 | tf_op jit(solution)/shard_map/ppermute | solution.py:25
  209.2 7.9 %collective-permute-start.6 = (f32[1,37,128]{2,0,1:T(1,128)S(1)}, f32[1,37,128]{2,0,1:T(1,128)S(1)}, u32[]{:S(2)}, u32[]{:S(2)}) collective-permute-start(f32[1,37,128]{2,0,1:T(1,128)S(1)} %get-tuple-element.56), channel_id=1, source_target_pairs={{0,1},{1,2},{2,3},{3,4},{4,5},{5,6},{6,7},{7,8},{8,9},{9,10},{10,1... | collective-permute-start | bytes 56840 | tf_op jit(solution)/shard_map/ppermute | solution.py:22
  213.2 5.1 collective-permute-start.5
  298.0 12.0 %collective-permute-start.8 = (f32[1,37,128]{2,0,1:T(1,128)S(1)}, f32[1,37,128]{2,0,1:T(1,128)S(1)}, u32[]{:S(2)}, u32[]{:S(2)}) collective-permute-start(f32[1,37,128]{2,0,1:T(1,128)S(1)} %get-tuple-element.50), channel_id=1, source_target_pairs={{0,16},{16,32},{32,48},{48,64},{64,80},{80,96},{96,112},{1,17},{17... | collective-permute-start | bytes 56840 | tf_op jit(solution)/shard_map/ppermute | solution.py:22
  300.5 9.6 %collective-permute-start.11 = (f32[1,37,128]{2,0,1:T(1,128)S(1)}, f32[1,37,128]{2,0,1:T(1,128)S(1)}, u32[]{:S(2)}, u32[]{:S(2)}) collective-permute-start(f32[1,37,128]{2,0,1:T(1,128)S(1)} %get-tuple-element.51), channel_id=1, source_target_pairs={{1,0},{2,1},{3,2},{4,3},{5,4},{6,5},{7,6},{8,7},{9,8},{10,9},{11,1... | collective-permute-start | bytes 56840 | tf_op jit(solution)/shard_map/ppermute | solution.py:25
  301.8 8.3 %collective-permute-start.10 = (f32[1,37,128]{2,0,1:T(1,128)S(1)}, f32[1,37,128]{2,0,1:T(1,128)S(1)}, u32[]{:S(2)}, u32[]{:S(2)}) collective-permute-start(f32[1,37,128]{2,0,1:T(1,128)S(1)} %get-tuple-element.52), channel_id=1, source_target_pairs={{0,1},{1,2},{2,3},{3,4},{4,5},{5,6},{6,7},{7,8},{8,9},{9,10},{10,1... | collective-permute-start | bytes 56840 | tf_op jit(solution)/shard_map/ppermute | solution.py:22
  305.8 5.1 collective-permute-start.9
  394.9 15.0 %collective-permute-start.16 = (f32[1,37,128]{2,0,1:T(1,128)S(1)}, f32[1,37,128]{2,0,1:T(1,128)S(1)}, u32[]{:S(2)}, u32[]{:S(2)}) collective-permute-start(f32[1,37,128]{2,0,1:T(1,128)S(1)} %get-tuple-element.42), channel_id=1, source_target_pairs={{0,16},{16,32},{32,48},{48,64},{64,80},{80,96},{96,112},{1,17},{17... | collective-permute-start | bytes 56840 | tf_op jit(solution)/shard_map/ppermute | solution.py:22
  397.3 13.9 %collective-permute-start.19 = (f32[1,37,128]{2,0,1:T(1,128)S(1)}, f32[1,37,128]{2,0,1:T(1,128)S(1)}, u32[]{:S(2)}, u32[]{:S(2)}) collective-permute-start(f32[1,37,128]{2,0,1:T(1,128)S(1)} %get-tuple-element.43), channel_id=1, source_target_pairs={{1,0},{2,1},{3,2},{4,3},{5,4},{6,5},{7,6},{8,7},{9,8},{10,9},{11,1... | collective-permute-start | bytes 56840 | tf_op jit(solution)/shard_map/ppermute | solution.py:25
  398.6 18.4 %collective-permute-start.18 = (f32[1,37,128]{2,0,1:T(1,128)S(1)}, f32[1,37,128]{2,0,1:T(1,128)S(1)}, u32[]{:S(2)}, u32[]{:S(2)}) collective-permute-start(f32[1,37,128]{2,0,1:T(1,128)S(1)} %get-tuple-element.44), channel_id=1, source_target_pairs={{0,1},{1,2},{2,3},{3,4},{4,5},{5,6},{6,7},{7,8},{8,9},{9,10},{10,1... | collective-permute-start | bytes 56840 | tf_op jit(solution)/shard_map/ppermute | solution.py:22
  402.6 16.5 %collective-permute-start.17 = (f32[1,37,128]{2,0,1:T(1,128)S(1)}, f32[1,37,128]{2,0,1:T(1,128)S(1)}, u32[]{:S(2)}, u32[]{:S(2)}) collective-permute-start(f32[1,37,128]{2,0,1:T(1,128)S(1)} %get-tuple-element.45), channel_id=1, source_target_pairs={{16,0},{32,16},{48,32},{64,48},{80,64},{96,80},{112,96},{17,1},{33... | collective-permute-start | bytes 56840 | tf_op jit(solution)/shard_map/ppermute | solution.py:25
  406.9 36.4 %collective-permute-start.12 = (f32[1,37,128]{2,0,1:T(1,128)S(1)}, f32[1,37,128]{2,0,1:T(1,128)S(1)}, u32[]{:S(2)}, u32[]{:S(2)}) collective-permute-start(f32[1,37,128]{2,0,1:T(1,128)S(1)} %get-tuple-element.46), channel_id=1, source_target_pairs={{0,16},{16,32},{32,48},{48,64},{64,80},{80,96},{96,112},{1,17},{17... | collective-permute-start | bytes 56840 | tf_op jit(solution)/shard_map/ppermute | solution.py:22
  409.9 33.4 %collective-permute-start.15 = (f32[1,37,128]{2,0,1:T(1,128)S(1)}, f32[1,37,128]{2,0,1:T(1,128)S(1)}, u32[]{:S(2)}, u32[]{:S(2)}) collective-permute-start(f32[1,37,128]{2,0,1:T(1,128)S(1)} %get-tuple-element.47), channel_id=1, source_target_pairs={{1,0},{2,1},{3,2},{4,3},{5,4},{6,5},{7,6},{8,7},{9,8},{10,9},{11,1... | collective-permute-start | bytes 56840 | tf_op jit(solution)/shard_map/ppermute | solution.py:25
  411.2 32.1 %collective-permute-start.14 = (f32[1,37,128]{2,0,1:T(1,128)S(1)}, f32[1,37,128]{2,0,1:T(1,128)S(1)}, u32[]{:S(2)}, u32[]{:S(2)}) collective-permute-start(f32[1,37,128]{2,0,1:T(1,128)S(1)} %get-tuple-element.48), channel_id=1, source_target_pairs={{0,1},{1,2},{2,3},{3,4},{4,5},{5,6},{6,7},{7,8},{8,9},{9,10},{10,1... | collective-permute-start | bytes 56840 | tf_op jit(solution)/shard_map/ppermute | solution.py:22
  417.0 26.4 %collective-permute-start.13 = (f32[1,37,128]{2,0,1:T(1,128)S(1)}, f32[1,37,128]{2,0,1:T(1,128)S(1)}, u32[]{:S(2)}, u32[]{:S(2)}) collective-permute-start(f32[1,37,128]{2,0,1:T(1,128)S(1)} %get-tuple-element.49), channel_id=1, source_target_pairs={{16,0},{32,16},{48,32},{64,48},{80,64},{96,80},{112,96},{17,1},{33... | collective-permute-start | bytes 56840 | tf_op jit(solution)/shard_map/ppermute | solution.py:25
  551.1 67.0 %all-to-all-start.1 = ((f32[128,1,576]{2,1,0:T(1,128)}), f32[128,1,576]{2,1,0:T(1,128)S(1)}, u32[]{:S(2)}, u32[]{:S(2)}) async-start(f32[128,1,576]{2,1,0:T(1,128)} %reshape.959), calls=%async_computation.1 | async-start | bytes 655360 | tf_op jit(solution)/shard_map/all_to_all | solution.py:147
  568.2 48.2 %copy-start.5 = (f32[3,20,1024]{2,1,0:T(8,128)S(1)}, f32[3,20,1024]{2,1,0:T(8,128)}, u32[]{:S(2)}) copy-start(f32[3,20,1024]{2,1,0:T(8,128)} %reshape.742) | copy-start | bytes 737284
  568.2 48.2 %copy-start.7 = (f32[3,20,1024]{2,1,0:T(8,128)S(1)}, f32[3,20,1024]{2,1,0:T(8,128)}, u32[]{:S(2)}) copy-start(f32[3,20,1024]{2,1,0:T(8,128)} %get-tuple-element.71) | copy-start | bytes 737284
  633.0 20.2 %all-to-all-start.2 = ((f32[128,1,384]{2,1,0:T(1,128)}), f32[128,1,384]{2,1,0:T(1,128)S(1)}, u32[]{:S(2)}, u32[]{:S(2)}) async-start(f32[128,1,384]{2,1,0:T(1,128)} %reshape.961), calls=%async_computation.2 | async-start | bytes 393216 | tf_op jit(solution)/shard_map/all_to_all | solution.py:165
  688.7 65.9 %copy-start.4 = (f32[3,20,1024]{2,1,0:T(8,128)S(1)}, f32[3,20,1024]{2,1,0:T(8,128)}, u32[]{:S(2)}) copy-start(f32[3,20,1024]{2,1,0:T(8,128)} %get-tuple-element.33) | copy-start | bytes 737284
  (18 other events, 579.9 us)
where the time goes:
time: 763 us; the launch traced here: 756 us
  local copies, waits for them, and re-layouts  523 us (69%)
  starting transfers between devices  95.3 us (12%)
  other arithmetic  88.9 us (12%)
  matrix products  41.6 us (5%)
    gather x10, local copies, waits for them, and re-layouts, face_flux(): other = table[:, :, links]  203 us
    gather x9, local copies, waits for them, and re-layouts, face_flux(): other_material = material_table[links]  115 us
    scatter-add x1, other arithmetic, on_device(): jnp.zeros((2, nodes, elems), jnp.float32).at[:, :, element].add(values)  65.1 us
    ppermute x10, starting transfers between devices, padded(): lax.ppermute(lax.slice_in_dim(block, block.shape[dim] - width, None, axis...  37.8 us
    gather x1, local copies, waits for them, and re-layouts, on_device(): interp = face_interp[:, face_kind, :]  37.4 us
    concatenate x5, local copies, waits for them, and re-layouts, face_flux(): table = jnp.concatenate([traces, arrived_traces], axis=-1)  36.8 us
    dot_general x1, matrix products, on_device(): jnp.einsum('qjn,cqj->cnj', interp, returned, precision=highest)  25.5 us
    gather x2, local copies, waits for them, and re-layouts, on_device(): traction = face_flux(solution, material, links, face_interp)[:, :, faces]  22.2 us
  transfers between devices with their start and end apart: 23, of which 3 were waited for; matrix products, arithmetic and copies ran while one was open for 24% of the time, Pallas kernels for 0%

commit v1 on v0

v1 whole, which is shorter than its diff:
```python
import functools

import jax
import jax.numpy as jnp
from jax import lax
from jax.experimental import pallas as pl
from jax.experimental.pallas import tpu as pltpu
from jax.sharding import PartitionSpec as P

ITERS = 4
NEWTON = 6
DAMPING = 0.5
TIME_STEP = 0.5
LOWER_EDGE = 0.25
UPPER_EDGE = 5.0
CENTER = 0.5 * (UPPER_EDGE + LOWER_EDGE)
SPREAD = 0.5 * (UPPER_EDGE - LOWER_EDGE)

MESH = pl.DeviceIdType.MESH
F32 = jnp.float32
BF16 = jnp.bfloat16
NT = (((1,), (1,)), ((), ()))

PA, PD = 8, 16
DEVS = PA * PD
ELEMS = 1024
ROWS = 40
BLOCK = 512
CHUNKS = 28
RANKS = 16


def coefficients():
    ratio = CENTER / SPREAD
    rho = 1.0 / ratio
    pairs = []
    for _ in range(ITERS):
        rho_next = 1.0 / (2.0 * ratio - rho)
        pairs.append((rho_next * rho, 2.0 * rho_next / SPREAD))
        rho = rho_next
    return pairs


def halves(value):
    high = value.astype(BF16)
    return high, (value - high.astype(F32)).astype(BF16)


def product(left, right):
    return jnp.dot(left, right, preferred_element_type=F32)


def onehot(digit, rows, columns):
    return (lax.broadcasted_iota(jnp.int32, (rows, columns), 0) == digit).astype(F32)


def choose(result, chunk, count, rows):
    width = result.shape[1]
    index = jnp.broadcast_to(chunk, (8, width))
    total = jnp.zeros((rows // 8, 8, width), F32)
    for s in range(count):
        part = result[s * rows : (s + 1) * rows].reshape(rows // 8, 8, width)
        total = jnp.where((index == s)[None], part, total)
    return total.reshape(rows, width)


def inverse_sinh(size, root):
    magnitude = jnp.log(jnp.abs(size) + root)
    return jnp.where(size < 0.0, -magnitude, magnitude)


def kernel(
    load, shear_ref, lame_ref, stiff_shear, stiff_lame, interp, links, count_ref, owner_ref, slot_ref, face_ref,
    normal_ref, friction_ref, state_ref, shear_load,
    disp_ref, residual_ref, rate_ref,
    weight, weights, lift_pair, field, stacked, trace, image, gathered, flux, flux_sum, alpha, table, hot_links,
    hot_owner, prefix, send_maps, face_maps, hot_send, hot_face, table_send, halo, pack, outbox, inbox, unpack,
    wide, hot_grid, pack_back, outbox_back, inbox_back, table_back,
    halo_send, halo_recv, go_send, go_recv, back_send, back_recv,
):
    along = lax.axis_index("along")
    depth = lax.axis_index("depth")
    me = along * PD + depth

    sides = (
        (0, 1, (along + 1, depth), along < PA - 1, along > 0),
        (1, 0, (along - 1, depth), along > 0, along < PA - 1),
        (2, 3, (along, depth + 1), depth < PD - 1, depth > 0),
        (3, 2, (along, depth - 1), depth > 0, depth < PD - 1),
    )

    for side, piece, target, sends, receives in sides:
        @pl.when(jnp.logical_not(receives))
        def _():
            halo[:, side] = jnp.zeros((ITERS, ROWS, 128), F32)

    weight[...] = jnp.zeros_like(weight)
    for f in range(4):
        for c in range(3):
            weight[f * ROWS + c * 12 : f * ROWS + c * 12 + 12, c * 20 : c * 20 + 20] = interp[:, f, :]
    weight[160:220, 0:60] = stiff_shear[...]
    weight[224:284, 0:60] = stiff_lame[...]
    whole = weight[:, 0:64]
    high = whole.astype(BF16).astype(F32)
    rest = whole - high
    lift_pair[0:128, 0:128] = jnp.transpose(weight[0:128, :])
    lift_pair[0:128, 128:256] = jnp.transpose(weight[128:256, :])
    weight[:, 64:128] = high
    weights[:, 0:64] = high
    weights[:, 64:128] = high
    weights[:, 128:192] = rest
    lifter, lifter_rest = halves(lift_pair[0:64, 0:160])
    matrix = weights[:, 0:192].astype(BF16)

    shear = shear_ref[...]
    lame = lame_ref[...]
    material = lame + 2.0 * shear
    inverse = 1.0 / material

    def lifted(ref):
        high, low = halves(ref[...])
        return product(lifter, high) + product(lifter_rest, high) + product(lifter, low)

    def build_links(b, carry):
        slots = links[b + b // 6]
        hot = onehot(jnp.bitwise_and(slots, 127), 128, BLOCK).astype(BF16)
        hot_links[b, 0:128, :] = hot
        hot_links[b, 128:256, :] = hot
        return carry

    lax.fori_loop(0, 7, build_links, 0)

    residual_ref[...] = load[...]
    field[60:64, :] = jnp.zeros((4, ELEMS), F32)
    field[0:60, :] = load[...] * (inverse * (1.0 / CENTER))
    disp_ref[...] = jnp.zeros_like(disp_ref)
    flux_sum[...] = jnp.zeros_like(flux_sum)

    def halo_copy(i, side, piece, target):
        return pltpu.make_async_remote_copy(
            src_ref=trace.at[120:160, piece * 128 : piece * 128 + 128],
            dst_ref=halo.at[i, side],
            send_sem=halo_send.at[i, side],
            recv_sem=halo_recv.at[i, side],
            device_id=target,
            device_id_type=MESH,
        )

    def step(i, first, scale_old, scale_new):
        now = field[...]
        high, low = halves(now)
        stacked[0:64, :] = high
        stacked[64:128, :] = low
        stacked[128:192, :] = high
        trace[...] = product(matrix[0:160], stacked[...])
        if first:
            for f in range(4):
                trace[f * ROWS + 36 : f * ROWS + 37, :] = material
        for side, piece, target, sends, receives in sides:
            @pl.when(sends)
            def _():
                halo_copy(i, side, piece, target).start()

        for p in range(CHUNKS // 2):
            parts = []
            for s in (2 * p, 2 * p + 1):
                t = s if s < 24 else s + 4
                f, j = t // 8, t % 8
                parts.append(trace[f * ROWS : (f + 1) * ROWS, j * 128 : (j + 1) * 128])
            high, low = halves(jnp.concatenate(parts, axis=0))
            table[p * 80 : p * 80 + 80, 0:128] = high
            table[p * 80 : p * 80 + 80, 128:256] = low

        def block(b, carry):
            place = b + b // 6
            chunk = lax.shift_right_logical(links[place], 7)
            chunk = jnp.where(chunk >= 24, chunk - 4, chunk)
            result = product(table[...], hot_links[b])
            f = place // 2
            half = place - 2 * f
            gathered[
                pl.ds(pl.multiple_of(f * ROWS, 8), ROWS), pl.ds(pl.multiple_of(half * BLOCK, BLOCK), BLOCK)
            ] = choose(result, chunk, CHUNKS, ROWS)
            return carry

        lax.fori_loop(0, 7, block, 0)

        volume = product(matrix[160:288], stacked[...])
        image[...] = shear * volume[0:64] + lame * volume[64:128]
        disp_ref[...] = disp_ref[...] + now[0:60]

        for side, piece, target, sends, receives in sides:
            @pl.when(receives)
            def _():
                halo_copy(i, side, piece, target).wait_recv()
            gathered[120:160, side * 128 : side * 128 + 128] = halo[i, side]

        if first:
            for f in range(4):
                alpha[f : f + 1, :] = 0.5 * (material + gathered[f * ROWS + 36 : f * ROWS + 37, :])
        for f in range(4):
            rows = slice(f * ROWS, (f + 1) * ROWS)
            value = alpha[f : f + 1, :] * (trace[rows, :] - gathered[rows, :])
            flux[rows, :] = value
            flux_sum[rows, :] = flux_sum[rows, :] + value
        left = residual_ref[...] - (image[...] + lifted(flux))[0:60]
        residual_ref[...] = left
        field[0:60, :] = scale_old * now[0:60] + scale_new * (left * inverse)
        for side, piece, target, sends, receives in sides:
            @pl.when(sends)
            def _():
                halo_copy(i, side, piece, target).wait_send()

    pairs = coefficients()
    step(0, True, *pairs[0])

    def later(i, carry):
        scale_old = jnp.where(i == 1, pairs[1][0], jnp.where(i == 2, pairs[2][0], pairs[3][0]))
        scale_new = jnp.where(i == 1, pairs[1][1], jnp.where(i == 2, pairs[2][1], pairs[3][1]))
        step(i, False, scale_old, scale_new)
        return carry

    lax.fori_loop(1, ITERS, later, 0)

    count = count_ref[...]
    lane = lax.broadcasted_iota(jnp.int32, (1, 128), 1)
    for t in range(RANKS):
        live = (lane + t * 128) < count
        owner = jnp.where(live, owner_ref[t], -1)
        hot_owner[t * 128 : (t + 1) * 128, :] = onehot(owner, 128, 128).astype(BF16)
    row = lax.broadcasted_iota(jnp.int32, (128, 256), 0)
    column = lax.broadcasted_iota(jnp.int32, (128, 256), 1)
    earlier = ((row < column) | (column >= 128)).astype(F32).astype(BF16)
    prefix[...] = product(hot_owner[...], earlier)
    base = jnp.zeros((128, 128), F32)
    sent = jnp.zeros((64, 128), F32)
    placed = jnp.zeros((64, 128), F32)
    for t in range(RANKS):
        rows = slice(t * 128, (t + 1) * 128)
        hot = hot_owner[rows, :]
        rank = jnp.sum(hot.astype(F32) * (prefix[rows, 0:128] + base), axis=0, keepdims=True)
        base = base + prefix[rows, 128:256]
        live = ((lane + t * 128) < count).astype(F32)
        rank_live = jnp.where(live > 0.0, rank, -1.0).astype(jnp.int32)
        face = face_ref[t]
        slot = slot_ref[t]
        face_high = lax.shift_right_logical(face, 7)
        face_low = jnp.bitwise_and(face, 127)
        ranks = onehot(rank_live, RANKS, 128)
        values = jnp.concatenate(
            [
                ranks * face_high.astype(F32),
                ranks * face_low.astype(F32),
                ranks * (lax.shift_right_logical(slot, 4) + 1).astype(F32),
                ranks * jnp.bitwise_and(slot, 15).astype(F32),
            ],
            axis=0,
        ).astype(BF16)
        sent = sent + lax.dot_general(values, hot, NT, preferred_element_type=F32)
        highs = onehot(face_high, 32, 128) * live
        values = jnp.concatenate([highs * (rank + 1.0), highs * owner_ref[t].astype(F32)], axis=0).astype(BF16)
        lows = onehot(face_low, 128, 128).astype(BF16)
        placed = placed + lax.dot_general(values, lows, NT, preferred_element_type=F32)
    send_maps[...] = sent
    face_maps[...] = placed

    for p in range(16):
        parts = []
        for s in (2 * p, 2 * p + 1):
            f, j = s // 8, s % 8
            parts.append(flux_sum[f * ROWS : (f + 1) * ROWS, j * 128 : (j + 1) * 128])
        high, low = halves(jnp.concatenate(parts, axis=0))
        table_send[p * 80 : p * 80 + 80, 0:128] = high
        table_send[p * 80 : p * 80 + 80, 128:256] = low
    for b in range(4):
        high = jnp.concatenate([send_maps[4 * b + j : 4 * b + j + 1, :] for j in range(4)], axis=1)
        low = jnp.concatenate([send_maps[16 + 4 * b + j : 17 + 4 * b + j, :] for j in range(4)], axis=1)
        hot = onehot(low.astype(jnp.int32), 128, BLOCK).astype(BF16)
        hot_send[0:128, :] = hot
        hot_send[128:256, :] = hot
        result = product(table_send[...], hot_send[...])
        chosen = choose(result, high.astype(jnp.int32), 32, ROWS)
        for j in range(4):
            rank = 4 * b + j
            pack[rank * ROWS : (rank + 1) * ROWS, :] = chosen[:, j * 128 : (j + 1) * 128]
            pack[rank * ROWS + 36 : rank * ROWS + 37, :] = (
                16.0 * send_maps[32 + rank : 33 + rank, :] + send_maps[48 + rank : 49 + rank, :] - 16.0
            )
    for j in range(5):
        outbox[pl.ds(j, 128, stride=8), :] = jnp.transpose(pack[j * 128 : (j + 1) * 128, :])

    def exchange(k, source, landing, size, send_sem, recv_sem):
        target = lax.rem(me + k, DEVS)
        return pltpu.make_async_remote_copy(
            src_ref=source.at[pl.ds(pl.multiple_of(target * 8, 8), size)],
            dst_ref=landing.at[pl.ds(pl.multiple_of(me * 8, 8), size)],
            send_sem=send_sem.at[k],
            recv_sem=recv_sem.at[k],
            device_id=(lax.div(target, PD), lax.rem(target, PD)),
            device_id_type=MESH,
        )

    def arrival(k, source, landing, size, send_sem, recv_sem):
        origin = lax.rem(me + DEVS - k, DEVS)
        return pltpu.make_async_remote_copy(
            src_ref=source.at[pl.ds(pl.multiple_of(origin * 8, 8), size)],
            dst_ref=landing.at[pl.ds(pl.multiple_of(origin * 8, 8), size)],
            send_sem=send_sem.at[k],
            recv_sem=recv_sem.at[k],
            device_id=(lax.div(origin, PD), lax.rem(origin, PD)),
            device_id_type=MESH,
        )

    def start_all(*what):
        def one(k, carry):
            exchange(k, *what).start()
            return carry

        lax.fori_loop(1, DEVS, one, 0)

    def receive_all(*what):
        def one(k, carry):
            arrival(k, *what).wait_recv()
            return carry

        lax.fori_loop(1, DEVS, one, 0)

    def sent_all(*what):
        def one(k, carry):
            exchange(k, *what).wait_send()
            return carry

        lax.fori_loop(1, DEVS, one, 0)

    go = (outbox, inbox, 5, go_send, go_recv)
    start_all(*go)
    mine = pl.ds(pl.multiple_of(me * 8, 8), 8)
    inbox[mine, :] = outbox[mine, :]

    def build_face(b, carry):
        low = jnp.concatenate([face_maps[pl.ds(32 + 4 * b + j, 1), :] for j in range(4)], axis=1)
        hot = onehot(low.astype(jnp.int32), 128, BLOCK).astype(BF16)
        hot_face[b, 0:128, :] = hot
        hot_face[b, 128:256, :] = hot
        return carry

    lax.fori_loop(0, 8, build_face, 0)

    receive_all(*go)
    for j in range(5):
        unpack[j * 128 : (j + 1) * 128, :] = jnp.transpose(inbox[pl.ds(j, 128, stride=8), :])
    for rank in range(RANKS):
        lanes = slice(rank * 128, (rank + 1) * 128)
        value = unpack[rank * ROWS : (rank + 1) * ROWS, :]
        high, low = halves(value)
        wide[0:40, lanes] = high.astype(F32)
        wide[40:80, lanes] = low.astype(F32)
        place = value[36:37, :].astype(jnp.int32)
        hot_grid[:, lanes] = onehot(place, BLOCK, 128).astype(BF16)
    both = lax.dot_general(wide[...].astype(BF16), hot_grid[...], NT, preferred_element_type=F32)
    traction = both[0:40] + both[40:80]

    state = state_ref[...]
    effective = normal_ref[...] * (1.0 + 0.5 * jnp.tanh(traction[24:36]))
    strike = shear_load[0] + traction[0:12]
    updip = shear_load[1] + traction[12:24]
    magnitude = jnp.sqrt(strike * strike + updip * updip)
    resist = friction_ref[...] * effective
    steep = resist * state
    velocity = magnitude / (DAMPING + steep)
    for _ in range(NEWTON - 1):
        scaled = state * velocity
        square = 1.0 + scaled * scaled
        inverse_root = lax.rsqrt(square)
        misfit = magnitude - DAMPING * velocity - resist * inverse_sinh(scaled, square * inverse_root)
        velocity = velocity + misfit / (DAMPING + steep * inverse_root)
    rate_ref[...] = velocity
    factor = TIME_STEP * velocity / jnp.maximum(magnitude, 1.0)
    slip = jnp.concatenate([factor * strike, factor * updip], axis=0)
    high = slip.astype(BF16).astype(F32)
    slip = jnp.concatenate([high, slip - high], axis=0).astype(BF16)
    out = product(slip, hot_grid[...])
    for rank in range(RANKS):
        lanes = slice(rank * 128, (rank + 1) * 128)
        pack_back[rank * 24 : (rank + 1) * 24, :] = out[0:24, lanes] + out[24:48, lanes]
    for j in range(3):
        outbox_back[pl.ds(j, 128, stride=8), :] = jnp.transpose(pack_back[j * 128 : (j + 1) * 128, :])
    back = (outbox_back, inbox_back, 3, back_send, back_recv)
    start_all(*back)
    inbox_back[mine, :] = outbox_back[mine, :]
    sent_all(*go)
    flux[...] = jnp.zeros_like(flux)
    receive_all(*back)

    for j in range(3):
        high, low = halves(jnp.transpose(inbox_back[pl.ds(j, 128, stride=8), :]))
        table_back[j * 128 : (j + 1) * 128, 0:128] = high
        table_back[j * 128 : (j + 1) * 128, 128:256] = low

    def place_back(b, carry):
        rank = jnp.concatenate([face_maps[pl.ds(4 * b + j, 1), :] for j in range(4)], axis=1)
        result = product(table_back[...], hot_face[b])
        f = b // 2
        half = b - 2 * f
        flux[
            pl.ds(pl.multiple_of(f * ROWS, 8), 24), pl.ds(pl.multiple_of(half * BLOCK, BLOCK), BLOCK)
        ] = choose(result, rank.astype(jnp.int32) - 1, RANKS, 24)
        return carry

    lax.fori_loop(0, 8, place_back, 0)
    disp_ref[...] = disp_ref[...] + 0.5 * lifted(flux)[0:60]
    sent_all(*back)


def on_device(
    right_side,
    shear_modulus,
    lame_lambda,
    stiff_shear,
    stiff_lame,
    face_interp,
    neighbours,
    fault_count,
    fault_owner,
    fault_slot,
    fault_face,
    normal_stress,
    friction,
    state_factor,
    shear_load,
):
    vmem = pl.BlockSpec(memory_space=pltpu.VMEM)
    scratch = [
        pltpu.VMEM((288, 128), F32),
        pltpu.VMEM((288, 256), F32),
        pltpu.VMEM((128, 256), F32),
        pltpu.VMEM((64, ELEMS), F32),
        pltpu.VMEM((192, ELEMS), BF16),
        pltpu.VMEM((160, ELEMS), F32),
        pltpu.VMEM((64, ELEMS), F32),
        pltpu.VMEM((160, ELEMS), F32),
        pltpu.VMEM((160, ELEMS), F32),
        pltpu.VMEM((160, ELEMS), F32),
        pltpu.VMEM((8, ELEMS), F32),
        pltpu.VMEM((CHUNKS * ROWS, 256), BF16),
        pltpu.VMEM((7, 256, BLOCK), BF16),
        pltpu.VMEM((2048, 128), BF16),
        pltpu.VMEM((2048, 256), F32),
        pltpu.VMEM((64, 128), F32),
        pltpu.VMEM((64, 128), F32),
        pltpu.VMEM((256, BLOCK), BF16),
        pltpu.VMEM((8, 256, BLOCK), BF16),
        pltpu.VMEM((32 * ROWS, 256), BF16),
        pltpu.VMEM((ITERS, 4, ROWS, 128), F32),
        pltpu.VMEM((640, 128), F32),
        pltpu.VMEM((1024, 128), F32),
        pltpu.VMEM((1024, 128), F32),
        pltpu.VMEM((640, 128), F32),
        pltpu.VMEM((80, 2048), F32),
        pltpu.VMEM((BLOCK, 2048), BF16),
        pltpu.VMEM((384, 128), F32),
        pltpu.VMEM((1024, 128), F32),
        pltpu.VMEM((1024, 128), F32),
        pltpu.VMEM((384, 256), BF16),
        pltpu.SemaphoreType.DMA((ITERS, 4)),
        pltpu.SemaphoreType.DMA((ITERS, 4)),
        pltpu.SemaphoreType.DMA((DEVS,)),
        pltpu.SemaphoreType.DMA((DEVS,)),
        pltpu.SemaphoreType.DMA((DEVS,)),
        pltpu.SemaphoreType.DMA((DEVS,)),
    ]
    displacement, residual, rate = pl.pallas_call(
        kernel,
        out_shape=(
            jax.ShapeDtypeStruct((60, ELEMS), F32),
            jax.ShapeDtypeStruct((60, ELEMS), F32),
            jax.ShapeDtypeStruct((12, 512), F32),
        ),
        in_specs=[vmem] * 15,
        out_specs=(vmem, vmem, vmem),
        scratch_shapes=scratch,
        compiler_params=pltpu.CompilerParams(has_side_effects=True, vmem_limit_bytes=48 * 2**20),
        name="window",
    )(
        right_side.reshape(60, ELEMS),
        shear_modulus.reshape(1, ELEMS),
        lame_lambda.reshape(1, ELEMS),
        stiff_shear,
        stiff_lame,
        face_interp,
        neighbours.reshape(8, 1, BLOCK),
        fault_count.reshape(1, 1),
        fault_owner.reshape(16, 1, 128),
        fault_slot.reshape(16, 1, 128),
        fault_face.reshape(16, 1, 128),
        normal_stress,
        friction,
        state_factor,
        shear_load,
    )
    return displacement.reshape(right_side.shape), residual.reshape(right_side.shape), rate


def solution(mesh):
    in_specs = (
        P(None, None, "along", "depth", None),
        P("along", "depth", None),
        P("along", "depth", None),
        P(),
        P(),
        P(),
        P("along", "depth", None),
        P("along", "depth"),
        P("along", "depth", None),
        P("along", "depth", None),
        P("along", "depth", None),
        P(None, ("along", "depth")),
        P(None, ("along", "depth")),
        P(None, ("along", "depth")),
        P(None, None, ("along", "depth")),
    )
    out_specs = (
        P(None, None, "along", "depth", None),
        P(None, None, "along", "depth", None),
        P(None, ("along", "depth")),
    )
    return jax.shard_map(
        on_device, mesh=mesh, in_specs=in_specs, out_specs=out_specs, check_vma=False
    )
```

time: 763 us -> 68.4 us (0.09)
  local copies, waits for them, and re-layouts: 523 us -> 4.14 us
  starting transfers between devices: 95.3 us -> 0 us
  other arithmetic: 88.9 us -> 1.53 us
  Pallas kernels: 0 us -> 61 us
  matrix products: 41.6 us -> 0 us
    gather x32 -> x0, local copies, waits for them, and re-layouts: 421 us -> none  [the longest x10 203 us: face_flux(): other = table[:, :, links]]
    scatter-add x1 -> x0, other arithmetic: 65.1 us -> none  [on_device(): jnp.zeros((2, nodes, elems), jnp.float32).at[:, :, element].add(values)]
    pallas_call x0 -> x1, Pallas kernels: none -> 61 us  [on_device(): pl.pallas_call(kernel, out_shape=(jax.ShapeDtypeStruct((60, ELEMS), F32),...]
    ppermute x20 -> x0, starting transfers between devices: 55.4 us -> none  [the longest x10 37.8 us: padded(): lax.ppermute(lax.slice_in_dim(block, block.shape[dim] - width, None, axis...]
    dot_general x14 -> x0, matrix products: 41.6 us -> none  [the longest x1 25.5 us: on_device(): jnp.einsum('qjn,cqj->cnj', interp, returned, precision=highest)]
    all_to_all x3 -> x0, starting transfers between devices: 39.9 us -> none  [the longest x1 17.1 us: on_device(): lax.all_to_all(send_traction, ('along', 'depth'), split_axis=1, concat_ax...]
    concatenate x6 -> x0, local copies, waits for them, and re-layouts: 36.8 us -> none  [the longest x5 36.8 us: face_flux(): table = jnp.concatenate([traces, arrived_traces], axis=-1)]
    unnamed x73 -> x26, local copies, waits for them, and re-layouts: 17.1 us -> 2.16 us
  transfers between devices with their start and end apart: 23 -> 0, of which waited for: 3 -> 0; matrix products, arithmetic and copies ran while one was open for 24% -> 0% of each run, Pallas kernels for 0% -> 0%
where the time goes in v1:
time: 68.4 us; the launch traced here: 68.1 us
  Pallas kernels  61 us (89%)
  local copies, waits for them, and re-layouts  4.14 us (6%)
  other arithmetic  1.53 us (2%)
  between operations  1.41 us (2%)
    pallas_call x1, Pallas kernels, on_device(): pl.pallas_call(kernel, out_shape=(jax.ShapeDtypeStruct((60, ELEMS), F32),...  61 us
    unnamed x26, local copies, waits for them, and re-layouts  2.16 us
    unnamed x1, other arithmetic  1.53 us

profile of v1, /device:TPU:1, one launch (start us, length us, event | category | flops | bytes accessed | tf_op | source)
XLA Modules:
  0.0 68.1 jit_solution(7124060401083030794)
XLA Ops:
  1.3 0.8 %copy.21.shear_load = f32[2,12,512]{2,1,0:T(8,128)S(1)} copy(f32[2,12,512]{2,0,1:T(2,128)} %param.29) | data formatting | bytes 98304 | tf_op args[14]
  2.1 1.5 %reduce = f32[3,20,1024]{2,1,0:T(8,128)S(1)} reduce(f32[3,20,1,1,1024]{4,3,2,1,0:T(1,128)} %param.15, f32[]{:T(128)} %constant.8), dimensions={2,3}, to_apply=%param.15.reduce_sub_computation | reduce | bytes 491524 | tf_op args[0]
  3.6 0.0 copy-start
  3.6 0.0 copy-start.1
  3.6 0.0 copy-start.2
  3.7 0.0 copy-start.3
  3.7 0.0 copy-start.4
  3.7 0.0 copy-start.5
  3.7 0.0 copy-start.6
  3.7 0.0 copy-start.7
  3.7 0.0 copy-start.8
  3.7 0.0 copy-start.9
  3.7 0.0 copy-start.10
  3.8 0.0 copy-start.11
  3.8 0.6 copy-done
  4.4 0.0 copy-done.1
  4.4 0.0 copy-done.2
  4.4 0.0 copy-done.3
  4.4 0.0 copy-done.4
  4.5 0.0 copy-done.5
  4.5 0.0 copy-done.6
  4.5 0.0 copy-done.7
  4.5 0.0 copy-done.8
  4.5 0.0 copy-done.9
  4.5 0.0 copy-done.10
  4.5 0.0 copy-done.11
  4.5 61.0 %window.1 = (f32[60,1024]{1,0:T(8,128)S(1)}, f32[60,1024]{1,0:T(8,128)S(1)}, f32[12,512]{1,0:T(8,128)S(1)}) custom-call(f32[60,1024]{1,0:T(8,128)S(1)} %reshape.33.load, f32[1,1024]{1,0:T(1,128)S(1)} %bitcast.10, f32[1,1024]{1,0:T(1,128)S(1)} %bitcast.11, f32[60,60]{1,0:T(8,128)S(1)} %copy-done, f32[60,60]{1,0:T(8,128)S(1)} %copy-done.1, ...), custom_call_target="tpu_custom_call" | custom-call | tf_op jit(solution)/shard_map/window/pallas_call | solution.py:472
  65.5 1.0 %reshape.42 = f32[3,20,1,1,1024]{4,3,2,1,0:T(1,128)} reshape(f32[60,1024]{1,0:T(8,128)S(1)} %get-tuple-element.6) | data formatting | bytes 491520 | tf_op jit(solution)/shard_map/reshape | solution.py:501
  66.5 1.0 %reshape.43 = f32[3,20,1,1,1024]{4,3,2,1,0:T(1,128)} reshape(f32[60,1024]{1,0:T(8,128)S(1)} %get-tuple-element.7) | data formatting | bytes 491520 | tf_op jit(solution)/shard_map/reshape | solution.py:501
  67.5 0.6 copy.27
  (1 shorter events, 0.0 us)
Async XLA Ops:
  3.6 0.8 %copy-start = (f32[60,60]{1,0:T(8,128)S(1)}, f32[60,60]{1,0:T(8,128)}, u32[]{:S(2)}) copy-start(f32[60,60]{1,0:T(8,128)} %stiff_shear.1) | copy-start | bytes 43204
  3.6 0.8 %copy-start.1 = (f32[60,60]{1,0:T(8,128)S(1)}, f32[60,60]{1,0:T(8,128)}, u32[]{:S(2)}) copy-start(f32[60,60]{1,0:T(8,128)} %stiff_lame.1) | copy-start | bytes 43204
  3.6 0.8 %copy-start.2 = (f32[12,512]{1,0:T(8,128)S(1)}, f32[12,512]{1,0:T(8,128)}, u32[]{:S(2)}) copy-start(f32[12,512]{1,0:T(8,128)} %normal_ref.1) | copy-start | bytes 73732
  3.7 0.8 %copy-start.3 = (f32[12,512]{1,0:T(8,128)S(1)}, f32[12,512]{1,0:T(8,128)}, u32[]{:S(2)}) copy-start(f32[12,512]{1,0:T(8,128)} %friction_ref.1) | copy-start | bytes 73732
  3.7 0.8 %copy-start.4 = (f32[12,512]{1,0:T(8,128)S(1)}, f32[12,512]{1,0:T(8,128)}, u32[]{:S(2)}) copy-start(f32[12,512]{1,0:T(8,128)} %state_ref.1) | copy-start | bytes 73732
  3.7 0.8 %copy-start.5 = (f32[12,4,20]{2,1,0:T(4,128)S(1)}, f32[12,4,20]{2,1,0:T(4,128)}, u32[]{:S(2)}) copy-start(f32[12,4,20]{2,1,0:T(4,128)} %interp.1) | copy-start | bytes 11524
  3.7 0.8 %copy-start.6 = (s32[1,1,4096]{2,1,0:T(1,128)S(1)}, s32[1,1,4096]{2,1,0:T(1,128)}, u32[]{:S(2)}) copy-start(s32[1,1,4096]{2,1,0:T(1,128)} %param.21) | copy-start | bytes 49156
  3.7 0.8 %copy-start.7 = (s32[1,1,2048]{2,1,0:T(1,128)S(1)}, s32[1,1,2048]{2,1,0:T(1,128)}, u32[]{:S(2)}) copy-start(s32[1,1,2048]{2,1,0:T(1,128)} %param.23) | copy-start | bytes 24580
  3.7 0.7 %copy-start.8 = (s32[1,1,2048]{2,1,0:T(1,128)S(1)}, s32[1,1,2048]{2,1,0:T(1,128)}, u32[]{:S(2)}) copy-start(s32[1,1,2048]{2,1,0:T(1,128)} %param.24) | copy-start | bytes 24580
  3.7 0.7 %copy-start.9 = (s32[1,1,2048]{2,1,0:T(1,128)S(1)}, s32[1,1,2048]{2,1,0:T(1,128)}, u32[]{:S(2)}) copy-start(s32[1,1,2048]{2,1,0:T(1,128)} %param.25) | copy-start | bytes 24580
  3.7 0.7 %copy-start.10 = (f32[1,1,1024]{2,1,0:T(1,128)S(1)}, f32[1,1,1024]{2,1,0:T(1,128)}, u32[]{:S(2)}) copy-start(f32[1,1,1024]{2,1,0:T(1,128)} %param.16) | copy-start | bytes 12292
  3.8 0.7 %copy-start.11 = (f32[1,1,1024]{2,1,0:T(1,128)S(1)}, f32[1,1,1024]{2,1,0:T(1,128)}, u32[]{:S(2)}) copy-start(f32[1,1,1024]{2,1,0:T(1,128)} %param.17) | copy-start | bytes 12292

commit v2 on v1

v2 whole, which is shorter than its diff:
```python
import functools

import jax
import jax.numpy as jnp
from jax import lax
from jax.experimental import pallas as pl
from jax.experimental.pallas import tpu as pltpu
from jax.sharding import PartitionSpec as P

ITERS = 4
NEWTON = 6
DAMPING = 0.5
TIME_STEP = 0.5
LOWER_EDGE = 0.25
UPPER_EDGE = 5.0
CENTER = 0.5 * (UPPER_EDGE + LOWER_EDGE)
SPREAD = 0.5 * (UPPER_EDGE - LOWER_EDGE)

MESH = pl.DeviceIdType.MESH
F32 = jnp.float32
BF16 = jnp.bfloat16
NT = (((1,), (1,)), ((), ()))

PA, PD = 8, 16
DEVS = PA * PD
ELEMS = 1024
ROWS = 40
BLOCK = 512
CHUNKS = 28
RANKS = 16


def coefficients():
    ratio = CENTER / SPREAD
    rho = 1.0 / ratio
    pairs = []
    for _ in range(ITERS):
        rho_next = 1.0 / (2.0 * ratio - rho)
        pairs.append((rho_next * rho, 2.0 * rho_next / SPREAD))
        rho = rho_next
    return pairs


def halves(value):
    high = value.astype(BF16)
    return high, (value - high.astype(F32)).astype(BF16)


def product(left, right):
    return jnp.dot(left, right, preferred_element_type=F32)


def onehot(digit, rows, columns):
    return (lax.broadcasted_iota(jnp.int32, (rows, columns), 0) == digit).astype(F32)


def choose(result, chunk, count, rows):
    width = result.shape[1]
    index = jnp.broadcast_to(chunk, (8, width))
    total = jnp.zeros((rows // 8, 8, width), F32)
    for s in range(count):
        part = result[s * rows : (s + 1) * rows].reshape(rows // 8, 8, width)
        total = jnp.where((index == s)[None], part, total)
    return total.reshape(rows, width)


def inverse_sinh(size, root):
    magnitude = jnp.log(jnp.abs(size) + root)
    return jnp.where(size < 0.0, -magnitude, magnitude)


def kernel(
    load, shear_ref, lame_ref, stiff_shear, stiff_lame, interp, links, count_ref, owner_ref, slot_ref, face_ref,
    normal_ref, friction_ref, state_ref, shear_load,
    disp_ref, residual_ref, rate_ref,
    weight, weights, lift_pair, solved, left_over, field, stacked, trace, image, gathered, flux, flux_sum, alpha,
    table, hot_links, hot_owner, prefix, send_maps, face_maps, hot_send, hot_face, table_send, halo, rims,
    ids_out, ids_one, ids_mid, ids_in, hot_grid, params_pack, params_out, params_one, params_mid, params_in, params,
    tractions, rate_pack, rate_out, rate_one, rate_mid, rate_in, wide, table_back,
    halo_send, halo_recv, ids_a, ids_b, ids_c, ids_d, par_a, par_b, par_c, par_d, rate_a, rate_b, rate_c, rate_d,
):
    along = lax.axis_index("along")
    depth = lax.axis_index("depth")

    barrier = pltpu.get_barrier_semaphore()
    for i in range(1, PA):
        pl.semaphore_signal(barrier, inc=1, device_id=(lax.rem(along + i, PA), depth), device_id_type=MESH)
    for i in range(1, PD):
        pl.semaphore_signal(barrier, inc=1, device_id=(along, lax.rem(depth + i, PD)), device_id_type=MESH)

    def row_copy(i, source, landing, size, sems, sending):
        peer = lax.rem(along + i, PA) if sending else lax.rem(along + PA - i, PA)
        place = along if sending else peer
        return pltpu.make_async_remote_copy(
            src_ref=source.at[pl.ds(pl.multiple_of(peer * size, 8), size)],
            dst_ref=landing.at[pl.ds(pl.multiple_of(place * size, 8), size)],
            send_sem=sems[0].at[i],
            recv_sem=sems[1].at[i],
            device_id=(peer, depth),
            device_id_type=MESH,
        )

    def column_copy(i, source, landing, size, sems, sending):
        peer = lax.rem(depth + i, PD) if sending else lax.rem(depth + PD - i, PD)
        place = depth if sending else peer
        return pltpu.make_async_remote_copy(
            src_ref=source.at[pl.ds(pl.multiple_of(peer * size, 8), size)],
            dst_ref=landing.at[pl.ds(pl.multiple_of(place * size, 8), size)],
            send_sem=sems[0].at[i],
            recv_sem=sems[1].at[i],
            device_id=(along, peer),
            device_id_type=MESH,
        )

    def go(kind, source, landing, size, sems):
        mine, peers = (along, PA) if kind is row_copy else (depth, PD)
        for i in range(1, peers):
            kind(i, source, landing, size, sems, True).start()
        own = pl.ds(pl.multiple_of(mine * size, 8), size)
        landing[own, :] = source[own, :]

    def arrive(kind, source, landing, size, sems):
        for i in range(1, PA if kind is row_copy else PD):
            kind(i, source, landing, size, sems, False).wait_recv()

    def drain(kind, source, landing, size, sems):
        for i in range(1, PA if kind is row_copy else PD):
            kind(i, source, landing, size, sems, True).wait_send()

    ids_first = (row_copy, ids_out, ids_one, 16, (ids_a, ids_b))
    ids_second = (column_copy, ids_mid, ids_in, 8, (ids_c, ids_d))
    params_first = (column_copy, params_out, params_one, 48, (par_a, par_b))
    params_second = (row_copy, params_mid, params_in, 96, (par_c, par_d))
    rate_first = (row_copy, rate_out, rate_one, 32, (rate_a, rate_b))
    rate_second = (column_copy, rate_mid, rate_in, 16, (rate_c, rate_d))

    count = count_ref[...]
    lane = lax.broadcasted_iota(jnp.int32, (1, 128), 1)
    for t in range(RANKS):
        live = (lane + t * 128) < count
        owner = jnp.where(live, owner_ref[t], -1)
        hot_owner[t * 128 : (t + 1) * 128, :] = onehot(owner, 128, 128).astype(BF16)
    row = lax.broadcasted_iota(jnp.int32, (128, 256), 0)
    column = lax.broadcasted_iota(jnp.int32, (128, 256), 1)
    earlier = ((row < column) | (column >= 128)).astype(F32).astype(BF16)
    prefix[...] = product(hot_owner[...], earlier)
    base = jnp.zeros((128, 128), F32)
    sent = jnp.zeros((64, 128), F32)
    placed = jnp.zeros((64, 128), F32)
    for t in range(RANKS):
        rows = slice(t * 128, (t + 1) * 128)
        hot = hot_owner[rows, :]
        rank = jnp.sum(hot.astype(F32) * (prefix[rows, 0:128] + base), axis=0, keepdims=True)
        base = base + prefix[rows, 128:256]
        live = ((lane + t * 128) < count).astype(F32)
        rank_live = jnp.where(live > 0.0, rank, -1.0).astype(jnp.int32)
        face = face_ref[t]
        slot = slot_ref[t]
        face_high = lax.shift_right_logical(face, 7)
        face_low = jnp.bitwise_and(face, 127)
        ranks = onehot(rank_live, RANKS, 128)
        values = jnp.concatenate(
            [
                ranks * face_high.astype(F32),
                ranks * face_low.astype(F32),
                ranks * (lax.shift_right_logical(slot, 4) + 1).astype(F32),
                ranks * jnp.bitwise_and(slot, 15).astype(F32),
            ],
            axis=0,
        ).astype(BF16)
        sent = sent + lax.dot_general(values, hot, NT, preferred_element_type=F32)
        highs = onehot(face_high, 32, 128) * live
        values = jnp.concatenate([highs * (rank + 1.0), highs * owner_ref[t].astype(F32)], axis=0).astype(BF16)
        lows = onehot(face_low, 128, 128).astype(BF16)
        placed = placed + lax.dot_general(values, lows, NT, preferred_element_type=F32)
    send_maps[...] = sent
    face_maps[...] = placed
    ids = 16.0 * sent[32:48] + sent[48:64] - 16.0
    ids_out[...] = jnp.transpose(jnp.concatenate([ids, jnp.zeros((112, 128), F32)], axis=0))

    pl.semaphore_wait(barrier, PA + PD - 2)
    go(*ids_first)

    sides = (
        (0, 1, (along + 1, depth), along < PA - 1, along > 0),
        (1, 0, (along - 1, depth), along > 0, along < PA - 1),
        (2, 3, (along, depth + 1), depth < PD - 1, depth > 0),
        (3, 2, (along, depth - 1), depth > 0, depth < PD - 1),
    )

    for side, piece, target, sends, receives in sides:
        @pl.when(jnp.logical_not(receives))
        def _():
            halo[:, side] = jnp.zeros((ITERS, ROWS, 128), F32)

    weight[...] = jnp.zeros_like(weight)
    for f in range(4):
        for c in range(3):
            weight[f * ROWS + c * 12 : f * ROWS + c * 12 + 12, c * 20 : c * 20 + 20] = interp[:, f, :]
    weight[160:220, 0:60] = stiff_shear[...]
    weight[224:284, 0:60] = stiff_lame[...]
    whole = weight[:, 0:64]
    high = whole.astype(BF16).astype(F32)
    rest = whole - high
    lift_pair[0:128, 0:128] = jnp.transpose(weight[0:128, :])
    lift_pair[0:128, 128:256] = jnp.transpose(weight[128:256, :])
    weights[:, 0:64] = high
    weights[:, 64:128] = high
    weights[:, 128:192] = rest
    lifter, lifter_rest = halves(lift_pair[0:64, 0:160])
    matrix = weights[:, 0:192].astype(BF16)

    shear = shear_ref[...]
    lame = lame_ref[...]
    material = lame + 2.0 * shear
    inverse = 1.0 / material

    def lifted(ref):
        high, low = halves(ref[...])
        return product(lifter, high) + product(lifter_rest, high) + product(lifter, low)

    def build_links(b, carry):
        slots = links[b + b // 6]
        hot = onehot(jnp.bitwise_and(slots, 127), 128, BLOCK).astype(BF16)
        hot_links[b, 0:128, :] = hot
        hot_links[b, 128:256, :] = hot
        return carry

    right = load[...].reshape(60, ELEMS)
    left_over[...] = right
    field[60:64, :] = jnp.zeros((4, ELEMS), F32)
    field[0:60, :] = right * (inverse * (1.0 / CENTER))
    solved[...] = jnp.zeros_like(solved)
    flux_sum[...] = jnp.zeros_like(flux_sum)

    def halo_copy(i, side, piece, target):
        return pltpu.make_async_remote_copy(
            src_ref=rims.at[i, piece],
            dst_ref=halo.at[i, side],
            send_sem=halo_send.at[i, side],
            recv_sem=halo_recv.at[i, side],
            device_id=target,
            device_id_type=MESH,
        )

    def step(i, scale_old, scale_new, between):
        first = i == 0
        now = field[...]
        high, low = halves(now)
        stacked[0:64, :] = high
        stacked[64:128, :] = low
        stacked[128:192, :] = high
        trace[...] = product(matrix[0:160], stacked[...])
        if first:
            for f in range(4):
                trace[f * ROWS + 36 : f * ROWS + 37, :] = material
        for side, piece, target, sends, receives in sides:
            rims[i, piece] = trace[120:160, piece * 128 : piece * 128 + 128]

            @pl.when(sends)
            def _():
                halo_copy(i, side, piece, target).start()

        if first:
            lax.fori_loop(0, 7, build_links, 0)

        for p in range(CHUNKS // 2):
            parts = []
            for s in (2 * p, 2 * p + 1):
                t = s if s < 24 else s + 4
                f, j = t // 8, t % 8
                parts.append(trace[f * ROWS : (f + 1) * ROWS, j * 128 : (j + 1) * 128])
            high, low = halves(jnp.concatenate(parts, axis=0))
            table[p * 80 : p * 80 + 80, 0:128] = high
            table[p * 80 : p * 80 + 80, 128:256] = low

        def block(b, carry):
            place = b + b // 6
            chunk = lax.shift_right_logical(links[place], 7)
            chunk = jnp.where(chunk >= 24, chunk - 4, chunk)
            result = product(table[...], hot_links[b])
            f = place // 2
            half = place - 2 * f
            gathered[
                pl.ds(pl.multiple_of(f * ROWS, 8), ROWS), pl.ds(pl.multiple_of(half * BLOCK, BLOCK), BLOCK)
            ] = choose(result, chunk, CHUNKS, ROWS)
            return carry

        lax.fori_loop(0, 7, block, 0)

        volume = product(matrix[160:288], stacked[...])
        image[...] = shear * volume[0:64] + lame * volume[64:128]
        solved[...] = solved[...] + now[0:60]
        between()

        for side, piece, target, sends, receives in sides:
            @pl.when(receives)
            def _():
                halo_copy(i, side, piece, target).wait_recv()
            gathered[120:160, side * 128 : side * 128 + 128] = halo[i, side]

        if first:
            for f in range(4):
                alpha[f : f + 1, :] = 0.5 * (material + gathered[f * ROWS + 36 : f * ROWS + 37, :])
        for f in range(4):
            rows = slice(f * ROWS, (f + 1) * ROWS)
            value = alpha[f : f + 1, :] * (trace[rows, :] - gathered[rows, :])
            flux[rows, :] = value
            flux_sum[rows, :] = flux_sum[rows, :] + value
        left = left_over[...] - (image[...] + lifted(flux))[0:60]
        left_over[...] = left
        if i < ITERS - 1:
            field[0:60, :] = scale_old * now[0:60] + scale_new * (left * inverse)

    def nothing():
        pass

    def ids_middle():
        arrive(*ids_first)
        for a in range(PA):
            ids_mid[pl.ds(a, PD, stride=PA), :] = ids_one[a * PD : (a + 1) * PD, :]
        go(*ids_second)

    def answer():
        arrive(*ids_second)
        asked = jnp.transpose(ids_in[...])[0:RANKS].astype(jnp.int32)
        for rank in range(RANKS):
            hot_grid[:, rank * 128 : (rank + 1) * 128] = onehot(asked[rank : rank + 1], BLOCK, 128).astype(BF16)
        owned = jnp.concatenate(
            [normal_ref[...] * friction_ref[...], state_ref[...], shear_load[0], shear_load[1]], axis=0
        )
        high = owned.astype(BF16).astype(F32)
        both = product(jnp.concatenate([high, owned - high], axis=0).astype(BF16), hot_grid[...])
        for rank in range(RANKS):
            lanes = slice(rank * 128, (rank + 1) * 128)
            params_pack[rank * 48 : (rank + 1) * 48, :] = both[0:48, lanes] + both[48:96, lanes]
        for j in range(6):
            params_out[pl.ds(j, 128, stride=6), :] = jnp.transpose(params_pack[j * 128 : (j + 1) * 128, :])
        go(*params_first)

    def params_middle():
        arrive(*params_first)
        for d in range(PD):
            for j in range(6):
                params_mid[pl.ds(d * 6 + j, PA, stride=96), :] = params_one[pl.ds(d * 48 + j, PA, stride=6), :]
        go(*params_second)

    pairs = coefficients()
    step(0, *pairs[0], nothing)
    ids_middle()
    step(1, *pairs[1], nothing)
    answer()
    step(2, *pairs[2], nothing)
    step(3, *pairs[3], params_middle)
    residual_ref[...] = left_over[...].reshape(60, 1, ELEMS)

    for p in range(16):
        parts = []
        for s in (2 * p, 2 * p + 1):
            f, j = s // 8, s % 8
            parts.append(flux_sum[f * ROWS : (f + 1) * ROWS, j * 128 : (j + 1) * 128])
        high, low = halves(jnp.concatenate(parts, axis=0))
        table_send[p * 80 : p * 80 + 80, 0:128] = high
        table_send[p * 80 : p * 80 + 80, 128:256] = low
    for b in range(4):
        high = jnp.concatenate([send_maps[4 * b + j : 4 * b + j + 1, :] for j in range(4)], axis=1)
        low = jnp.concatenate([send_maps[16 + 4 * b + j : 17 + 4 * b + j, :] for j in range(4)], axis=1)
        hot = onehot(low.astype(jnp.int32), 128, BLOCK).astype(BF16)
        hot_send[0:128, :] = hot
        hot_send[128:256, :] = hot
        result = product(table_send[...], hot_send[...])
        tractions[b] = choose(result, high.astype(jnp.int32), 32, ROWS)

    def build_face(b, carry):
        low = jnp.concatenate([face_maps[pl.ds(32 + 4 * b + j, 1), :] for j in range(4)], axis=1)
        hot = onehot(low.astype(jnp.int32), 128, BLOCK).astype(BF16)
        hot_face[b, 0:128, :] = hot
        hot_face[b, 128:256, :] = hot
        return carry

    lax.fori_loop(0, 8, build_face, 0)
    rate_pack[...] = jnp.zeros_like(rate_pack)

    arrive(*params_second)
    for j in range(6):
        params[j * 128 : (j + 1) * 128, :] = jnp.transpose(params_in[pl.ds(j, 128, stride=6), :])
    for b in range(4):
        first = [params[(4 * b + j) * 48 : (4 * b + j + 1) * 48, :] for j in range(4)]
        owned = jnp.concatenate(first, axis=1)
        traction = tractions[b]
        state = owned[12:24]
        strike = owned[24:36] + traction[0:12]
        updip = owned[36:48] + traction[12:24]
        magnitude = jnp.sqrt(strike * strike + updip * updip)
        resist = owned[0:12] * (1.0 + 0.5 * jnp.tanh(traction[24:36]))
        steep = resist * state
        velocity = magnitude / (DAMPING + steep)
        for _ in range(NEWTON - 1):
            scaled = state * velocity
            square = 1.0 + scaled * scaled
            inverse_root = lax.rsqrt(square)
            misfit = magnitude - DAMPING * velocity - resist * inverse_sinh(scaled, square * inverse_root)
            velocity = velocity + misfit / (DAMPING + steep * inverse_root)
        factor = TIME_STEP * velocity / jnp.maximum(magnitude, 1.0)
        slip = jnp.concatenate([factor * strike, factor * updip], axis=0)
        for j in range(4):
            rank = 4 * b + j
            rate_pack[rank * 16 : rank * 16 + 12, :] = velocity[:, j * 128 : (j + 1) * 128]
        for j in (0, 2):
            parts = [slip[:, j * 128 : (j + 1) * 128], slip[:, (j + 1) * 128 : (j + 2) * 128]]
            high, low = halves(jnp.concatenate(parts, axis=0))
            at = (4 * b + j) * 24
            table_back[at : at + 48, 0:128] = high
            table_back[at : at + 48, 128:256] = low
    for j in range(2):
        rate_out[pl.ds(j, 128, stride=2), :] = jnp.transpose(rate_pack[j * 128 : (j + 1) * 128, :])
    go(*rate_first)

    flux[...] = jnp.zeros_like(flux)

    def place_back(b, carry):
        rank = jnp.concatenate([face_maps[pl.ds(4 * b + j, 1), :] for j in range(4)], axis=1)
        result = product(table_back[...], hot_face[b])
        f = b // 2
        half = b - 2 * f
        flux[
            pl.ds(pl.multiple_of(f * ROWS, 8), 24), pl.ds(pl.multiple_of(half * BLOCK, BLOCK), BLOCK)
        ] = choose(result, rank.astype(jnp.int32) - 1, RANKS, 24)
        return carry

    lax.fori_loop(0, 8, place_back, 0)

    arrive(*rate_first)
    for a in range(PA):
        for j in range(2):
            rate_mid[pl.ds(a * 2 + j, PD, stride=16), :] = rate_one[pl.ds(a * 32 + j, PD, stride=2), :]
    go(*rate_second)
    disp_ref[...] = (solved[...] + 0.5 * lifted(flux)[0:60]).reshape(60, 1, ELEMS)
    for each in (ids_first, ids_second, params_first, params_second, rate_first):
        drain(*each)
    for i in range(ITERS):
        for side, piece, target, sends, receives in sides:
            @pl.when(sends)
            def _():
                halo_copy(i, side, piece, target).wait_send()

    arrive(*rate_second)
    for j in range(2):
        value = jnp.transpose(rate_in[pl.ds(j, 128, stride=2), :])
        high = value.astype(BF16).astype(F32)
        low = value - high
        for r in range(8):
            lanes = slice((8 * j + r) * 128, (8 * j + r + 1) * 128)
            wide[0:16, lanes] = high[r * 16 : (r + 1) * 16]
            wide[16:32, lanes] = low[r * 16 : (r + 1) * 16]
    both = lax.dot_general(wide[...].astype(BF16), hot_grid[...], NT, preferred_element_type=F32)
    rate_ref[...] = both[0:12] + both[16:28]
    drain(*rate_second)


def on_device(
    right_side,
    shear_modulus,
    lame_lambda,
    stiff_shear,
    stiff_lame,
    face_interp,
    neighbours,
    fault_count,
    fault_owner,
    fault_slot,
    fault_face,
    normal_stress,
    friction,
    state_factor,
    shear_load,
):
    vmem = pl.BlockSpec(memory_space=pltpu.VMEM)
    scratch = [
        pltpu.VMEM((288, 128), F32),
        pltpu.VMEM((288, 256), F32),
        pltpu.VMEM((128, 256), F32),
        pltpu.VMEM((60, ELEMS), F32),
        pltpu.VMEM((60, ELEMS), F32),
        pltpu.VMEM((64, ELEMS), F32),
        pltpu.VMEM((192, ELEMS), BF16),
        pltpu.VMEM((160, ELEMS), F32),
        pltpu.VMEM((64, ELEMS), F32),
        pltpu.VMEM((160, ELEMS), F32),
        pltpu.VMEM((160, ELEMS), F32),
        pltpu.VMEM((160, ELEMS), F32),
        pltpu.VMEM((8, ELEMS), F32),
        pltpu.VMEM((CHUNKS * ROWS, 256), BF16),
        pltpu.VMEM((7, 256, BLOCK), BF16),
        pltpu.VMEM((2048, 128), BF16),
        pltpu.VMEM((2048, 256), F32),
        pltpu.VMEM((64, 128), F32),
        pltpu.VMEM((64, 128), F32),
        pltpu.VMEM((256, BLOCK), BF16),
        pltpu.VMEM((8, 256, BLOCK), BF16),
        pltpu.VMEM((32 * ROWS, 256), BF16),
        pltpu.VMEM((ITERS, 4, ROWS, 128), F32),
        pltpu.VMEM((ITERS, 4, ROWS, 128), F32),
        pltpu.VMEM((128, 128), F32),
        pltpu.VMEM((128, 128), F32),
        pltpu.VMEM((128, 128), F32),
        pltpu.VMEM((128, 128), F32),
        pltpu.VMEM((BLOCK, 2048), BF16),
        pltpu.VMEM((768, 128), F32),
        pltpu.VMEM((768, 128), F32),
        pltpu.VMEM((768, 128), F32),
        pltpu.VMEM((768, 128), F32),
        pltpu.VMEM((768, 128), F32),
        pltpu.VMEM((768, 128), F32),
        pltpu.VMEM((4, ROWS, BLOCK), F32),
        pltpu.VMEM((256, 128), F32),
        pltpu.VMEM((256, 128), F32),
        pltpu.VMEM((256, 128), F32),
        pltpu.VMEM((256, 128), F32),
        pltpu.VMEM((256, 128), F32),
        pltpu.VMEM((32, 2048), F32),
        pltpu.VMEM((384, 256), BF16),
        pltpu.SemaphoreType.DMA((ITERS, 4)),
        pltpu.SemaphoreType.DMA((ITERS, 4)),
    ] + [pltpu.SemaphoreType.DMA((PD,))] * 12
    displacement, residual, rate = pl.pallas_call(
        kernel,
        out_shape=(
            jax.ShapeDtypeStruct((60, 1, ELEMS), F32),
            jax.ShapeDtypeStruct((60, 1, ELEMS), F32),
            jax.ShapeDtypeStruct((12, 512), F32),
        ),
        in_specs=[vmem] * 15,
        out_specs=(vmem, vmem, vmem),
        scratch_shapes=scratch,
        compiler_params=pltpu.CompilerParams(collective_id=0, has_side_effects=True, vmem_limit_bytes=48 * 2**20),
        name="window",
    )(
        right_side.reshape(60, 1, ELEMS),
        shear_modulus.reshape(1, ELEMS),
        lame_lambda.reshape(1, ELEMS),
        stiff_shear,
        stiff_lame,
        face_interp,
        neighbours.reshape(8, 1, BLOCK),
        fault_count.reshape(1, 1),
        fault_owner.reshape(16, 1, 128),
        fault_slot.reshape(16, 1, 128),
        fault_face.reshape(16, 1, 128),
        normal_stress,
        friction,
        state_factor,
        shear_load,
    )
    return displacement.reshape(right_side.shape), residual.reshape(right_side.shape), rate


def solution(mesh):
    in_specs = (
        P(None, None, "along", "depth", None),
        P("along", "depth", None),
        P("along", "depth", None),
        P(),
        P(),
        P(),
        P("along", "depth", None),
        P("along", "depth"),
        P("along", "depth", None),
        P("along", "depth", None),
        P("along", "depth", None),
        P(None, ("along", "depth")),
        P(None, ("along", "depth")),
        P(None, ("along", "depth")),
        P(None, None, ("along", "depth")),
    )
    out_specs = (
        P(None, None, "along", "depth", None),
        P(None, None, "along", "depth", None),
        P(None, ("along", "depth")),
    )
    return jax.shard_map(
        on_device, mesh=mesh, in_specs=in_specs, out_specs=out_specs, check_vma=False
    )
```

time: 68.4 us -> 58.5 us (0.86)
  Pallas kernels: 61 us -> 47.8 us
  local copies, waits for them, and re-layouts: 4.14 us -> 8.81 us
  other arithmetic: 1.53 us -> 0 us
    pallas_call x1, Pallas kernels: 61 us -> 47.8 us  [on_device(): pl.pallas_call(kernel, out_shape=(jax.ShapeDtypeStruct((60, 1, ELEMS), F3...]
    unnamed x26 -> x30, local copies, waits for them, and re-layouts: 2.16 us -> 8.81 us
    reshape x3 -> x0, local copies, waits for them, and re-layouts: 1.98 us -> none  [the longest x1 0.98 us: on_device(): displacement.reshape(right_side.shape)]
    unnamed x1 -> x0, other arithmetic: 1.53 us -> none
where the time goes in v2:
time: 58.5 us; the launch traced here: 57.9 us
  Pallas kernels  47.8 us (82%)
  local copies, waits for them, and re-layouts  8.81 us (15%)
  between operations  1.39 us (2%)
    pallas_call x1, Pallas kernels, on_device(): pl.pallas_call(kernel, out_shape=(jax.ShapeDtypeStruct((60, 1, ELEMS), F3...  47.8 us
    unnamed x30, local copies, waits for them, and re-layouts  8.81 us

profile of v2, /device:TPU:1, one launch (start us, length us, event | category | flops | bytes accessed | tf_op | source)
XLA Modules:
  0.0 57.9 jit_solution(1571882326652153343)
XLA Ops:
  1.3 0.0 copy-start.11
  1.3 0.0 copy-start.6
  1.3 0.0 copy-start.1
  1.3 0.0 copy-start.2
  1.3 0.0 copy-start.3
  1.3 0.8 %copy.18.shear_load = f32[2,12,512]{2,1,0:T(8,128)S(1)} copy(f32[2,12,512]{2,0,1:T(2,128)} %param.29) | data formatting | bytes 98304 | tf_op args[14]
  2.2 0.0 copy-done.11
  2.2 0.0 copy-done.6
  2.2 0.0 copy-done.1
  2.2 0.0 copy-done.2
  2.2 0.0 copy-done.3
  2.2 0.0 copy-start
  2.2 0.9 %copy-done = f32[3,20,1,1,1024]{4,3,2,1,0:T(1,128)S(1)} copy-done((f32[3,20,1,1,1024]{4,3,2,1,0:T(1,128)S(1)}, f32[3,20,1,1,1024]{4,3,2,1,0:T(1,128)}, u32[]{:S(2)}) %copy-start) | copy-done | bytes 245784
  3.2 0.0 copy-start.4
  3.2 0.8 %copy-done.4 = f32[12,512]{1,0:T(8,128)S(1)} copy-done((f32[12,512]{1,0:T(8,128)S(1)}, f32[12,512]{1,0:T(8,128)}, u32[]{:S(2)}) %copy-start.4) | copy-done | bytes 24600
  3.9 0.0 copy-start.5
  3.9 0.8 %copy-done.5 = f32[12,512]{1,0:T(8,128)S(1)} copy-done((f32[12,512]{1,0:T(8,128)S(1)}, f32[12,512]{1,0:T(8,128)}, u32[]{:S(2)}) %copy-start.5) | copy-done | bytes 24600
  4.7 0.0 copy-start.7
  4.7 0.7 %copy-done.7 = s32[1,1,4096]{2,1,0:T(1,128)S(1)} copy-done((s32[1,1,4096]{2,1,0:T(1,128)S(1)}, s32[1,1,4096]{2,1,0:T(1,128)}, u32[]{:S(2)}) %copy-start.7) | copy-done | bytes 16408
  5.4 0.0 copy-start.8
  5.4 0.7 %copy-done.8 = s32[1,1,2048]{2,1,0:T(1,128)S(1)} copy-done((s32[1,1,2048]{2,1,0:T(1,128)S(1)}, s32[1,1,2048]{2,1,0:T(1,128)}, u32[]{:S(2)}) %copy-start.8) | copy-done | bytes 8216
  6.1 0.0 copy-start.9
  6.1 0.7 %copy-done.9 = s32[1,1,2048]{2,1,0:T(1,128)S(1)} copy-done((s32[1,1,2048]{2,1,0:T(1,128)S(1)}, s32[1,1,2048]{2,1,0:T(1,128)}, u32[]{:S(2)}) %copy-start.9) | copy-done | bytes 8216
  6.8 0.0 copy-start.10
  6.8 0.7 %copy-done.10 = s32[1,1,2048]{2,1,0:T(1,128)S(1)} copy-done((s32[1,1,2048]{2,1,0:T(1,128)S(1)}, s32[1,1,2048]{2,1,0:T(1,128)}, u32[]{:S(2)}) %copy-start.10) | copy-done | bytes 8216
  7.5 0.0 copy-start.12
  7.5 0.7 %copy-done.12 = f32[1,1,1024]{2,1,0:T(1,128)S(1)} copy-done((f32[1,1,1024]{2,1,0:T(1,128)S(1)}, f32[1,1,1024]{2,1,0:T(1,128)}, u32[]{:S(2)}) %copy-start.12) | copy-done | bytes 4120
  8.2 47.8 %window.1 = (f32[60,1,1024]{2,1,0:T(1,128)S(1)}, f32[60,1,1024]{2,1,0:T(1,128)S(1)}, f32[12,512]{1,0:T(8,128)S(1)}) custom-call(f32[60,1,1024]{2,1,0:T(1,128)S(1)} %bitcast.13, f32[1,1024]{1,0:T(1,128)S(1)} %bitcast.20, f32[1,1024]{1,0:T(1,128)S(1)} %bitcast.21, f32[60,60]{1,0:T(8,128)S(1)} %copy-done.1, f32[60,60]{1,0:T(8,128)S(1)} %copy-done.2, ...), custom_call_target="tpu_custom_call" | custom-call | tf_op jit(solution)/shard_map/window/pallas_call | solution.py:526
  55.9 0.7 %copy.25 = f32[3,20,1,1,1024]{4,3,2,1,0:T(1,128)} copy(f32[3,20,1,1,1024]{4,3,2,1,0:T(1,128)S(1)} %bitcast.15) | data formatting | bytes 491520
  56.6 0.7 %copy.26 = f32[3,20,1,1,1024]{4,3,2,1,0:T(1,128)} copy(f32[3,20,1,1,1024]{4,3,2,1,0:T(1,128)S(1)} %bitcast.14) | data formatting | bytes 491520
  57.3 0.6 %copy.27 = f32[12,512]{1,0:T(8,128)} copy(f32[12,512]{1,0:T(8,128)S(1)} %get-tuple-element.17) | data formatting | bytes 49152
Async XLA Ops:
  1.3 0.9 %copy-start.11 = (f32[1,1,1024]{2,1,0:T(1,128)S(1)}, f32[1,1,1024]{2,1,0:T(1,128)}, u32[]{:S(2)}) copy-start(f32[1,1,1024]{2,1,0:T(1,128)} %param.16) | copy-start | bytes 12292
  1.3 0.9 %copy-start.6 = (f32[12,4,20]{2,1,0:T(4,128)S(1)}, f32[12,4,20]{2,1,0:T(4,128)}, u32[]{:S(2)}) copy-start(f32[12,4,20]{2,1,0:T(4,128)} %interp.1) | copy-start | bytes 11524
  1.3 0.9 %copy-start.1 = (f32[60,60]{1,0:T(8,128)S(1)}, f32[60,60]{1,0:T(8,128)}, u32[]{:S(2)}) copy-start(f32[60,60]{1,0:T(8,128)} %stiff_shear.1) | copy-start | bytes 43204
  1.3 0.9 %copy-start.2 = (f32[60,60]{1,0:T(8,128)S(1)}, f32[60,60]{1,0:T(8,128)}, u32[]{:S(2)}) copy-start(f32[60,60]{1,0:T(8,128)} %stiff_lame.1) | copy-start | bytes 43204
  1.3 0.9 %copy-start.3 = (f32[12,512]{1,0:T(8,128)S(1)}, f32[12,512]{1,0:T(8,128)}, u32[]{:S(2)}) copy-start(f32[12,512]{1,0:T(8,128)} %normal_ref.1) | copy-start | bytes 73732
  2.2 0.9 %copy-start = (f32[3,20,1,1,1024]{4,3,2,1,0:T(1,128)S(1)}, f32[3,20,1,1,1024]{4,3,2,1,0:T(1,128)}, u32[]{:S(2)}) copy-start(f32[3,20,1,1,1024]{4,3,2,1,0:T(1,128)} %param.15) | copy-start | bytes 737284
  3.2 0.8 %copy-start.4 = (f32[12,512]{1,0:T(8,128)S(1)}, f32[12,512]{1,0:T(8,128)}, u32[]{:S(2)}) copy-start(f32[12,512]{1,0:T(8,128)} %friction_ref.1) | copy-start | bytes 73732
  3.9 0.8 %copy-start.5 = (f32[12,512]{1,0:T(8,128)S(1)}, f32[12,512]{1,0:T(8,128)}, u32[]{:S(2)}) copy-start(f32[12,512]{1,0:T(8,128)} %state_ref.1) | copy-start | bytes 73732
  4.7 0.7 %copy-start.7 = (s32[1,1,4096]{2,1,0:T(1,128)S(1)}, s32[1,1,4096]{2,1,0:T(1,128)}, u32[]{:S(2)}) copy-start(s32[1,1,4096]{2,1,0:T(1,128)} %param.21) | copy-start | bytes 49156
  5.4 0.7 %copy-start.8 = (s32[1,1,2048]{2,1,0:T(1,128)S(1)}, s32[1,1,2048]{2,1,0:T(1,128)}, u32[]{:S(2)}) copy-start(s32[1,1,2048]{2,1,0:T(1,128)} %param.23) | copy-start | bytes 24580
  6.1 0.7 %copy-start.9 = (s32[1,1,2048]{2,1,0:T(1,128)S(1)}, s32[1,1,2048]{2,1,0:T(1,128)}, u32[]{:S(2)}) copy-start(s32[1,1,2048]{2,1,0:T(1,128)} %param.24) | copy-start | bytes 24580
  6.8 0.7 %copy-start.10 = (s32[1,1,2048]{2,1,0:T(1,128)S(1)}, s32[1,1,2048]{2,1,0:T(1,128)}, u32[]{:S(2)}) copy-start(s32[1,1,2048]{2,1,0:T(1,128)} %param.25) | copy-start | bytes 24580
  7.5 0.7 %copy-start.12 = (f32[1,1,1024]{2,1,0:T(1,128)S(1)}, f32[1,1,1024]{2,1,0:T(1,128)}, u32[]{:S(2)}) copy-start(f32[1,1,1024]{2,1,0:T(1,128)} %param.17) | copy-start | bytes 12292

commit v3 on v2

--- a/solution.py
+++ b/solution.py
@@ -70,9 +70,11 @@
 
 
 def kernel(
-    load, shear_ref, lame_ref, stiff_shear, stiff_lame, interp, links, count_ref, owner_ref, slot_ref, face_ref,
-    normal_ref, friction_ref, state_ref, shear_load,
+    count_ref, load_hbm, shear_hbm, lame_hbm, stiff_shear_hbm, stiff_lame_hbm, interp_hbm, links_hbm, owner_hbm,
+    slot_hbm, face_hbm, normal_hbm, friction_hbm, state_hbm, shear_load_hbm,
     disp_ref, residual_ref, rate_ref,
+    load, shear_ref, lame_ref, stiff_shear, stiff_lame, interp, links, owner_ref, slot_ref, face_ref,
+    normal_ref, friction_ref, state_ref, shear_load, fetch_sem,
     weight, weights, lift_pair, solved, left_over, field, stacked, trace, image, gathered, flux, flux_sum, alpha,
     table, hot_links, hot_owner, prefix, send_maps, face_maps, hot_send, hot_face, table_send, halo, rims,
     ids_out, ids_one, ids_mid, ids_in, hot_grid, params_pack, params_out, params_one, params_mid, params_in, params,
@@ -81,6 +83,18 @@
 ):
     along = lax.axis_index("along")
     depth = lax.axis_index("depth")
+
+    operands = (
+        (owner_hbm, owner_ref), (slot_hbm, slot_ref), (face_hbm, face_ref), (load_hbm, load), (shear_hbm, shear_ref),
+        (lame_hbm, lame_ref), (stiff_shear_hbm, stiff_shear), (stiff_lame_hbm, stiff_lame), (interp_hbm, interp),
+        (links_hbm, links), (normal_hbm, normal_ref), (friction_hbm, friction_ref), (state_hbm, state_ref),
+        (shear_load_hbm, shear_load),
+    )
+    fetches = [
+        pltpu.make_async_copy(source, target, fetch_sem.at[i]) for i, (source, target) in enumerate(operands)
+    ]
+    for fetch in fetches:
+        fetch.start()
 
     barrier = pltpu.get_barrier_semaphore()
     for i in range(1, PA):
@@ -134,6 +148,8 @@
     rate_first = (row_copy, rate_out, rate_one, 32, (rate_a, rate_b))
     rate_second = (column_copy, rate_mid, rate_in, 16, (rate_c, rate_d))
 
+    for fetch in fetches[0:3]:
+        fetch.wait()
     count = count_ref[...]
     lane = lax.broadcasted_iota(jnp.int32, (1, 128), 1)
     for t in range(RANKS):
@@ -193,6 +209,8 @@
         def _():
             halo[:, side] = jnp.zeros((ITERS, ROWS, 128), F32)
 
+    for fetch in fetches[3:]:
+        fetch.wait()
     weight[...] = jnp.zeros_like(weight)
     for f in range(4):
         for c in range(3):
@@ -327,7 +345,7 @@
         for rank in range(RANKS):
             hot_grid[:, rank * 128 : (rank + 1) * 128] = onehot(asked[rank : rank + 1], BLOCK, 128).astype(BF16)
         owned = jnp.concatenate(
-            [normal_ref[...] * friction_ref[...], state_ref[...], shear_load[0], shear_load[1]], axis=0
+            [normal_ref[...] * friction_ref[...], state_ref[...], shear_load[:, 0, :], shear_load[:, 1, :]], axis=0
         )
         high = owned.astype(BF16).astype(F32)
         both = product(jnp.concatenate([high, owned - high], axis=0).astype(BF16), hot_grid[...])
@@ -346,10 +364,8 @@
         go(*params_second)
 
     pairs = coefficients()
-    step(0, *pairs[0], nothing)
-    ids_middle()
-    step(1, *pairs[1], nothing)
-    answer()
+    step(0, *pairs[0], ids_middle)
+    step(1, *pairs[1], answer)
     step(2, *pairs[2], nothing)
     step(3, *pairs[3], params_middle)
     residual_ref[...] = left_over[...].reshape(60, 1, ELEMS)
@@ -476,7 +492,23 @@
     shear_load,
 ):
     vmem = pl.BlockSpec(memory_space=pltpu.VMEM)
+    hbm = pl.BlockSpec(memory_space=pltpu.HBM)
     scratch = [
+        pltpu.VMEM((60, 1, ELEMS), F32),
+        pltpu.VMEM((1, ELEMS), F32),
+        pltpu.VMEM((1, ELEMS), F32),
+        pltpu.VMEM((60, 60), F32),
+        pltpu.VMEM((60, 60), F32),
+        pltpu.VMEM((12, 4, 20), F32),
+        pltpu.VMEM((8, 1, BLOCK), jnp.int32),
+        pltpu.VMEM((16, 1, 128), jnp.int32),
+        pltpu.VMEM((16, 1, 128), jnp.int32),
+        pltpu.VMEM((16, 1, 128), jnp.int32),
+        pltpu.VMEM((12, 512), F32),
+        pltpu.VMEM((12, 512), F32),
+        pltpu.VMEM((12, 512), F32),
+        pltpu.VMEM((12, 2, 512), F32),
+        pltpu.SemaphoreType.DMA((14,)),
         pltpu.VMEM((288, 128), F32),
         pltpu.VMEM((288, 256), F32),
         pltpu.VMEM((128, 256), F32),
@@ -530,12 +562,13 @@
             jax.ShapeDtypeStruct((60, 1, ELEMS), F32),
             jax.ShapeDtypeStruct((12, 512), F32),
         ),
-        in_specs=[vmem] * 15,
+        in_specs=[vmem] + [hbm] * 14,
         out_specs=(vmem, vmem, vmem),
         scratch_shapes=scratch,
-        compiler_params=pltpu.CompilerParams(collective_id=0, has_side_effects=True, vmem_limit_bytes=48 * 2**20),
+        compiler_params=pltpu.CompilerParams(collective_id=0, has_side_effects=True, vmem_limit_bytes=64000 * 1024),
         name="window",
     )(
+        fault_count.reshape(1, 1),
         right_side.reshape(60, 1, ELEMS),
         shear_modulus.reshape(1, ELEMS),
         lame_lambda.reshape(1, ELEMS),
@@ -543,14 +576,13 @@
         stiff_lame,
         face_interp,
         neighbours.reshape(8, 1, BLOCK),
-        fault_count.reshape(1, 1),
         fault_owner.reshape(16, 1, 128),
         fault_slot.reshape(16, 1, 128),
         fault_face.reshape(16, 1, 128),
         normal_stress,
         friction,
         state_factor,
-        shear_load,
+        shear_load.transpose(1, 0, 2),
     )
     return displacement.reshape(right_side.shape), residual.reshape(right_side.shape), rate
 

time: 58.5 us -> 53.5 us (0.915)
  local copies, waits for them, and re-layouts: 8.81 us -> 3.07 us
  Pallas kernels: 47.8 us -> 49 us
    unnamed x30 -> x7, local copies, waits for them, and re-layouts: 8.81 us -> 3.07 us
    pallas_call x1, Pallas kernels: 47.8 us -> 49 us  [on_device(): pl.pallas_call(kernel, out_shape=(jax.ShapeDtypeStruct((60, 1, ELEMS), F3...]
where the time goes in v3:
time: 53.5 us; the launch traced here: 53.3 us
  Pallas kernels  49 us (92%)
  local copies, waits for them, and re-layouts  3.07 us (6%)
  between operations  1.3 us (2%)
    pallas_call x1, Pallas kernels, on_device(): pl.pallas_call(kernel, out_shape=(jax.ShapeDtypeStruct((60, 1, ELEMS), F3...  49 us
    unnamed x7, local copies, waits for them, and re-layouts  3.07 us

profile of v3, /device:TPU:1, one launch (start us, length us, event | category | flops | bytes accessed | tf_op | source)
XLA Modules:
  0.0 53.3 jit_solution(15941355513491945206)
XLA Ops:
  1.3 49.0 %window.1 = (f32[60,1,1024]{2,1,0:T(1,128)}, f32[60,1,1024]{2,1,0:T(1,128)}, f32[12,512]{1,0:T(8,128)}) custom-call(s32[1,1]{1,0:T(1,128)S(6)} %copy.23.count_ref, f32[60,1,1024]{2,1,0:T(1,128)} %bitcast.14, f32[1,1024]{1,0:T(1,128)} %bitcast.22, f32[1,1024]{1,0:T(1,128)} %bitcast.23, f32[60,60]{1,0:T(8,128)} %stiff_shear_hbm.1, f32[60,60]{1,0:T(8,128)} %stiff_lame_hbm.1, ...), custom_call_target="tpu_custom_call" | custom-call | tf_op jit(solution)/shard_map/window/pallas_call | solution.py:558
  50.2 0.0 copy-start
  50.3 1.7 %copy.24 = f32[3,20,1,1,1024]{4,3,2,1,0:T(1,128)} copy(f32[3,20,1,1,1024]{4,3,2,1,0:T(1,128)} %bitcast.16) | data formatting | bytes 491520
  51.9 0.0 copy-done
  52.0 0.0 copy-start.1
  52.0 0.7 %copy.25 = f32[3,20,1,1,1024]{4,3,2,1,0:T(1,128)} copy(f32[3,20,1,1,1024]{4,3,2,1,0:T(1,128)S(1)} %bitcast.15) | data formatting | bytes 491520
  52.6 0.1 copy-done.1
  52.7 0.6 %copy.26 = f32[12,512]{1,0:T(8,128)} copy(f32[12,512]{1,0:T(8,128)S(1)} %copy-done.1) | data formatting | bytes 49152
Async XLA Ops:
  50.2 1.7 %copy-start = (f32[60,1,1024]{2,1,0:T(1,128)S(1)}, f32[60,1,1024]{2,1,0:T(1,128)}, u32[]{:S(2)}) copy-start(f32[60,1,1024]{2,1,0:T(1,128)} %get-tuple-element.7) | copy-start | bytes 737284
  52.0 0.8 %copy-start.1 = (f32[12,512]{1,0:T(8,128)S(1)}, f32[12,512]{1,0:T(8,128)}, u32[]{:S(2)}) copy-start(f32[12,512]{1,0:T(8,128)} %get-tuple-element.17) | copy-start | bytes 73732

commit v4 on v3

--- a/solution.py
+++ b/solution.py
@@ -72,14 +72,17 @@
 def kernel(
     count_ref, load_hbm, shear_hbm, lame_hbm, stiff_shear_hbm, stiff_lame_hbm, interp_hbm, links_hbm, owner_hbm,
     slot_hbm, face_hbm, normal_hbm, friction_hbm, state_hbm, shear_load_hbm,
-    disp_ref, residual_ref, rate_ref,
+    disp_hbm, residual_hbm, rate_hbm,
+    disp_ref, residual_ref, rate_ref, result_sem,
     load, shear_ref, lame_ref, stiff_shear, stiff_lame, interp, links, owner_ref, slot_ref, face_ref,
     normal_ref, friction_ref, state_ref, shear_load, fetch_sem,
     weight, weights, lift_pair, solved, left_over, field, stacked, trace, image, gathered, flux, flux_sum, alpha,
     table, hot_links, hot_owner, prefix, send_maps, face_maps, hot_send, hot_face, table_send, halo, rims,
-    ids_out, ids_one, ids_mid, ids_in, hot_grid, params_pack, params_out, params_one, params_mid, params_in, params,
+    ids_out, ids_one, ids_mid, ids_in, hot_grid, params_pack, down_out, down_one, down_mid, down_in, over_out,
+    over_one, over_mid, over_in, params,
     tractions, rate_pack, rate_out, rate_one, rate_mid, rate_in, wide, table_back,
-    halo_send, halo_recv, ids_a, ids_b, ids_c, ids_d, par_a, par_b, par_c, par_d, rate_a, rate_b, rate_c, rate_d,
+    halo_send, halo_recv, ids_a, ids_b, ids_c, ids_d, par_a, par_b, par_c, par_d, par_e, par_f, par_g, par_h,
+    rate_a, rate_b, rate_c, rate_d,
 ):
     along = lax.axis_index("along")
     depth = lax.axis_index("depth")
@@ -96,6 +99,13 @@
     for fetch in fetches:
         fetch.start()
 
+    results = [
+        pltpu.make_async_copy(source, target, result_sem.at[i])
+        for i, (source, target) in enumerate(
+            ((residual_ref, residual_hbm), (disp_ref, disp_hbm), (rate_ref, rate_hbm))
+        )
+    ]
+
     barrier = pltpu.get_barrier_semaphore()
     for i in range(1, PA):
         pl.semaphore_signal(barrier, inc=1, device_id=(lax.rem(along + i, PA), depth), device_id_type=MESH)
@@ -143,8 +153,10 @@
 
     ids_first = (row_copy, ids_out, ids_one, 16, (ids_a, ids_b))
     ids_second = (column_copy, ids_mid, ids_in, 8, (ids_c, ids_d))
-    params_first = (column_copy, params_out, params_one, 48, (par_a, par_b))
-    params_second = (row_copy, params_mid, params_in, 96, (par_c, par_d))
+    down_first = (column_copy, down_out, down_one, 24, (par_a, par_b))
+    down_second = (row_copy, down_mid, down_in, 48, (par_c, par_d))
+    over_first = (row_copy, over_out, over_one, 48, (par_e, par_f))
+    over_second = (column_copy, over_mid, over_in, 24, (par_g, par_h))
     rate_first = (row_copy, rate_out, rate_one, 32, (rate_a, rate_b))
     rate_second = (column_copy, rate_mid, rate_in, 16, (rate_c, rate_d))
 
@@ -261,7 +273,7 @@
             device_id_type=MESH,
         )
 
-    def step(i, scale_old, scale_new, between):
+    def step(i, scale_old, scale_new, before, between):
         first = i == 0
         now = field[...]
         high, low = halves(now)
@@ -279,6 +291,7 @@
             def _():
                 halo_copy(i, side, piece, target).start()
 
+        before()
         if first:
             lax.fori_loop(0, 7, build_links, 0)
 
@@ -352,23 +365,34 @@
         for rank in range(RANKS):
             lanes = slice(rank * 128, (rank + 1) * 128)
             params_pack[rank * 48 : (rank + 1) * 48, :] = both[0:48, lanes] + both[48:96, lanes]
-        for j in range(6):
-            params_out[pl.ds(j, 128, stride=6), :] = jnp.transpose(params_pack[j * 128 : (j + 1) * 128, :])
-        go(*params_first)
+        for j in range(3):
+            down_out[pl.ds(j, 128, stride=3), :] = jnp.transpose(params_pack[j * 128 : (j + 1) * 128, :])
+        go(*down_first)
+        for j in range(3):
+            turned = jnp.transpose(params_pack[(3 + j) * 128 : (4 + j) * 128, :])
+            for d in range(PD):
+                over_out[pl.ds(d * 3 + j, PA, stride=48), :] = turned[d * PA : (d + 1) * PA]
+        go(*over_first)
 
     def params_middle():
-        arrive(*params_first)
+        arrive(*down_first)
         for d in range(PD):
-            for j in range(6):
-                params_mid[pl.ds(d * 6 + j, PA, stride=96), :] = params_one[pl.ds(d * 48 + j, PA, stride=6), :]
-        go(*params_second)
+            for j in range(3):
+                down_mid[pl.ds(d * 3 + j, PA, stride=48), :] = down_one[pl.ds(d * 24 + j, PA, stride=3), :]
+        go(*down_second)
+        arrive(*over_first)
+        for a in range(PA):
+            for j in range(3):
+                over_mid[pl.ds(a * 3 + j, PD, stride=24), :] = over_one[pl.ds(a * 48 + j, PD, stride=3), :]
+        go(*over_second)
 
     pairs = coefficients()
-    step(0, *pairs[0], ids_middle)
-    step(1, *pairs[1], answer)
-    step(2, *pairs[2], nothing)
-    step(3, *pairs[3], params_middle)
+    step(0, *pairs[0], nothing, ids_middle)
+    step(1, *pairs[1], nothing, answer)
+    step(2, *pairs[2], nothing, nothing)
+    step(3, *pairs[3], params_middle, nothing)
     residual_ref[...] = left_over[...].reshape(60, 1, ELEMS)
+    results[0].start()
 
     for p in range(16):
         parts = []
@@ -397,9 +421,13 @@
     lax.fori_loop(0, 8, build_face, 0)
     rate_pack[...] = jnp.zeros_like(rate_pack)
 
-    arrive(*params_second)
-    for j in range(6):
-        params[j * 128 : (j + 1) * 128, :] = jnp.transpose(params_in[pl.ds(j, 128, stride=6), :])
+    arrive(*down_second)
+    for j in range(3):
+        params[j * 128 : (j + 1) * 128, :] = jnp.transpose(down_in[pl.ds(j, 128, stride=3), :])
+    arrive(*over_second)
+    for j in range(3):
+        parts = [over_in[pl.ds(a * 3 + j, PD, stride=24), :] for a in range(PA)]
+        params[(3 + j) * 128 : (4 + j) * 128, :] = jnp.transpose(jnp.concatenate(parts, axis=0))
     for b in range(4):
         first = [params[(4 * b + j) * 48 : (4 * b + j + 1) * 48, :] for j in range(4)]
         owned = jnp.concatenate(first, axis=1)
@@ -452,7 +480,8 @@
             rate_mid[pl.ds(a * 2 + j, PD, stride=16), :] = rate_one[pl.ds(a * 32 + j, PD, stride=2), :]
     go(*rate_second)
     disp_ref[...] = (solved[...] + 0.5 * lifted(flux)[0:60]).reshape(60, 1, ELEMS)
-    for each in (ids_first, ids_second, params_first, params_second, rate_first):
+    results[1].start()
+    for each in (ids_first, ids_second, down_first, down_second, over_first, over_second, rate_first):
         drain(*each)
     for i in range(ITERS):
         for side, piece, target, sends, receives in sides:
@@ -471,7 +500,23 @@
             wide[16:32, lanes] = low[r * 16 : (r + 1) * 16]
     both = lax.dot_general(wide[...].astype(BF16), hot_grid[...], NT, preferred_element_type=F32)
     rate_ref[...] = both[0:12] + both[16:28]
+    results[2].start()
     drain(*rate_second)
+    for result in results:
+        result.wait()
+
+
+def hand_over(disp_ref, residual_ref, rate_ref, disp_out, residual_out, rate_out, disp, residual, rate, sems):
+    ways = ((disp_ref, disp, disp_out), (residual_ref, residual, residual_out), (rate_ref, rate, rate_out))
+    inward = [pltpu.make_async_copy(way[0], way[1], sems.at[0, i]) for i, way in enumerate(ways)]
+    outward = [pltpu.make_async_copy(way[1], way[2], sems.at[1, i]) for i, way in enumerate(ways)]
+    for copy in inward:
+        copy.start()
+    for first, second in zip(inward, outward):
+        first.wait()
+        second.start()
+    for copy in outward:
+        copy.wait()
 
 
 def on_device(
@@ -494,6 +539,10 @@
     vmem = pl.BlockSpec(memory_space=pltpu.VMEM)
     hbm = pl.BlockSpec(memory_space=pltpu.HBM)
     scratch = [
+        pltpu.VMEM((60, 1, ELEMS), F32),
+        pltpu.VMEM((60, 1, ELEMS), F32),
+        pltpu.VMEM((12, 512), F32),
+        pltpu.SemaphoreType.DMA((3,)),
         pltpu.VMEM((60, 1, ELEMS), F32),
         pltpu.VMEM((1, ELEMS), F32),
         pltpu.VMEM((1, ELEMS), F32),
@@ -539,10 +588,14 @@
         pltpu.VMEM((128, 128), F32),
         pltpu.VMEM((BLOCK, 2048), BF16),
         pltpu.VMEM((768, 128), F32),
-        pltpu.VMEM((768, 128), F32),
-        pltpu.VMEM((768, 128), F32),
-        pltpu.VMEM((768, 128), F32),
-        pltpu.VMEM((768, 128), F32),
+        pltpu.VMEM((384, 128), F32),
+        pltpu.VMEM((384, 128), F32),
+        pltpu.VMEM((384, 128), F32),
+        pltpu.VMEM((384, 128), F32),
+        pltpu.VMEM((384, 128), F32),
+        pltpu.VMEM((384, 128), F32),
+        pltpu.VMEM((384, 128), F32),
+        pltpu.VMEM((384, 128), F32),
         pltpu.VMEM((768, 128), F32),
         pltpu.VMEM((4, ROWS, BLOCK), F32),
         pltpu.VMEM((256, 128), F32),
@@ -554,7 +607,7 @@
         pltpu.VMEM((384, 256), BF16),
         pltpu.SemaphoreType.DMA((ITERS, 4)),
         pltpu.SemaphoreType.DMA((ITERS, 4)),
-    ] + [pltpu.SemaphoreType.DMA((PD,))] * 12
+    ] + [pltpu.SemaphoreType.DMA((PD,))] * 16
     displacement, residual, rate = pl.pallas_call(
         kernel,
         out_shape=(
@@ -563,7 +616,7 @@
             jax.ShapeDtypeStruct((12, 512), F32),
         ),
         in_specs=[vmem] + [hbm] * 14,
-        out_specs=(vmem, vmem, vmem),
+        out_specs=(hbm, hbm, hbm),
         scratch_shapes=scratch,
         compiler_params=pltpu.CompilerParams(collective_id=0, has_side_effects=True, vmem_limit_bytes=64000 * 1024),
         name="window",
@@ -584,6 +637,24 @@
         state_factor,
         shear_load.transpose(1, 0, 2),
     )
+    displacement, residual, rate = pl.pallas_call(
+        hand_over,
+        out_shape=(
+            jax.ShapeDtypeStruct((480, 128), F32),
+            jax.ShapeDtypeStruct((480, 128), F32),
+            jax.ShapeDtypeStruct((12, 512), F32),
+        ),
+        in_specs=[hbm] * 3,
+        out_specs=(hbm, hbm, hbm),
+        scratch_shapes=[
+            pltpu.VMEM((480, 128), F32),
+            pltpu.VMEM((480, 128), F32),
+            pltpu.VMEM((12, 512), F32),
+            pltpu.SemaphoreType.DMA((2, 3)),
+        ],
+        compiler_params=pltpu.CompilerParams(vmem_limit_bytes=64000 * 1024),
+        name="hand_over",
+    )(displacement.reshape(480, 128), residual.reshape(480, 128), rate)
     return displacement.reshape(right_side.shape), residual.reshape(right_side.shape), rate
 
 

time: 53.5 us -> 47.9 us (0.90)
  local copies, waits for them, and re-layouts: 3.07 us -> 0 us
  Pallas kernels: 49 us -> 46.5 us
    pallas_call x1, Pallas kernels: 49 us -> 44.7 us  [on_device(): pl.pallas_call(kernel, out_shape=(jax.ShapeDtypeStruct((60, 1, ELEMS), F3...]
    unnamed x7 -> x0, local copies, waits for them, and re-layouts: 3.07 us -> none
    pallas_call x0 -> x1, Pallas kernels: none -> 1.81 us  [on_device(): pl.pallas_call(hand_over, out_shape=(jax.ShapeDtypeStruct((480, 128), F32...]
where the time goes in v4:
time: 47.9 us; the launch traced here: 47.8 us
  Pallas kernels  46.5 us (97%)
  between operations  1.29 us (3%)
    pallas_call x1, Pallas kernels, on_device(): pl.pallas_call(kernel, out_shape=(jax.ShapeDtypeStruct((60, 1, ELEMS), F3...  44.7 us
    pallas_call x1, Pallas kernels, on_device(): pl.pallas_call(hand_over, out_shape=(jax.ShapeDtypeStruct((480, 128), F32...  1.81 us

profile of v4, /device:TPU:1, one launch (start us, length us, event | category | flops | bytes accessed | tf_op | source)
XLA Modules:
  0.0 47.8 jit_solution(2811723722907466909)
XLA Ops:
  1.3 44.7 %window.1 = (f32[60,1,1024]{2,1,0:T(1,128)}, f32[60,1,1024]{2,1,0:T(1,128)}, f32[12,512]{1,0:T(8,128)}) custom-call(s32[1,1]{1,0:T(1,128)S(6)} %copy.22.count_ref, f32[60,1,1024]{2,1,0:T(1,128)} %bitcast.12, f32[1,1024]{1,0:T(1,128)} %bitcast.20, f32[1,1024]{1,0:T(1,128)} %bitcast.21, f32[60,60]{1,0:T(8,128)} %stiff_shear_hbm.1, f32[60,60]{1,0:T(8,128)} %stiff_lame_hbm.1, ...), custom_call_target="tpu_custom_call" | custom-call | tf_op jit(solution)/shard_map/window/pallas_call | solution.py:611
  45.9 1.8 %hand_over.1 = (f32[480,128]{1,0:T(8,128)}, f32[480,128]{1,0:T(8,128)}, f32[12,512]{1,0:T(8,128)}) custom-call(f32[480,128]{1,0:T(8,128)} %bitcast.13, f32[480,128]{1,0:T(8,128)} %bitcast.14, f32[12,512]{1,0:T(8,128)} %get-tuple-element.11.rate_ref), custom_call_target="tpu_custom_call" | custom-call | tf_op jit(solution)/shard_map/hand_over/pallas_call | solution.py:640

commit v5 on v4

--- a/solution.py
+++ b/solution.py
@@ -27,6 +27,7 @@
 ROWS = 40
 BLOCK = 512
 CHUNKS = 28
+SPLIT = 18
 RANKS = 16
 
 
@@ -96,7 +97,7 @@
     fetches = [
         pltpu.make_async_copy(source, target, fetch_sem.at[i]) for i, (source, target) in enumerate(operands)
     ]
-    for fetch in fetches:
+    for fetch in fetches[0:3]:
         fetch.start()
 
     results = [
@@ -111,6 +112,9 @@
         pl.semaphore_signal(barrier, inc=1, device_id=(lax.rem(along + i, PA), depth), device_id_type=MESH)
     for i in range(1, PD):
         pl.semaphore_signal(barrier, inc=1, device_id=(along, lax.rem(depth + i, PD)), device_id_type=MESH)
+
+    for fetch in fetches[3:]:
+        fetch.start()
 
     def row_copy(i, source, landing, size, sems, sending):
         peer = lax.rem(along + i, PA) if sending else lax.rem(along + PA - i, PA)
@@ -174,7 +178,7 @@
     prefix[...] = product(hot_owner[...], earlier)
     base = jnp.zeros((128, 128), F32)
     sent = jnp.zeros((64, 128), F32)
-    placed = jnp.zeros((64, 128), F32)
+    ranked = []
     for t in range(RANKS):
         rows = slice(t * 128, (t + 1) * 128)
         hot = hot_owner[rows, :]
@@ -197,17 +201,23 @@
             axis=0,
         ).astype(BF16)
         sent = sent + lax.dot_general(values, hot, NT, preferred_element_type=F32)
-        highs = onehot(face_high, 32, 128) * live
-        values = jnp.concatenate([highs * (rank + 1.0), highs * owner_ref[t].astype(F32)], axis=0).astype(BF16)
-        lows = onehot(face_low, 128, 128).astype(BF16)
-        placed = placed + lax.dot_general(values, lows, NT, preferred_element_type=F32)
+        ranked.append((rank, live))
     send_maps[...] = sent
-    face_maps[...] = placed
     ids = 16.0 * sent[32:48] + sent[48:64] - 16.0
     ids_out[...] = jnp.transpose(jnp.concatenate([ids, jnp.zeros((112, 128), F32)], axis=0))
 
     pl.semaphore_wait(barrier, PA + PD - 2)
     go(*ids_first)
+
+    placed = jnp.zeros((64, 128), F32)
+    for t in range(RANKS):
+        rank, live = ranked[t]
+        face = face_ref[t]
+        highs = onehot(lax.shift_right_logical(face, 7), 32, 128) * live
+        values = jnp.concatenate([highs * (rank + 1.0), highs * owner_ref[t].astype(F32)], axis=0).astype(BF16)
+        lows = onehot(jnp.bitwise_and(face, 127), 128, 128).astype(BF16)
+        placed = placed + lax.dot_general(values, lows, NT, preferred_element_type=F32)
+    face_maps[...] = placed
 
     sides = (
         (0, 1, (along + 1, depth), along < PA - 1, along > 0),
@@ -239,6 +249,8 @@
     weights[:, 128:192] = rest
     lifter, lifter_rest = halves(lift_pair[0:64, 0:160])
     matrix = weights[:, 0:192].astype(BF16)
+    rim_matrix = weights[120:160, 0:192].astype(BF16)
+    rim_lifter, rim_rest = halves(lift_pair[0:64, 120:160])
 
     shear = shear_ref[...]
     lame = lame_ref[...]
@@ -273,29 +285,31 @@
             device_id_type=MESH,
         )
 
-    def step(i, scale_old, scale_new, before, between):
+    def step(i, scale_old, scale_new, split, middle, between):
         first = i == 0
         now = field[...]
         high, low = halves(now)
         stacked[0:64, :] = high
         stacked[64:128, :] = low
         stacked[128:192, :] = high
+        rim = product(rim_matrix, stacked[:, 0:BLOCK])
+        for side, piece, target, sends, receives in sides:
+            rims[i, piece] = rim[:, piece * 128 : piece * 128 + 128]
+            if first:
+                rims[i, piece, 36:37, :] = material[:, piece * 128 : piece * 128 + 128]
+
+            @pl.when(sends)
+            def _():
+                halo_copy(i, side, piece, target).start()
+
         trace[...] = product(matrix[0:160], stacked[...])
         if first:
             for f in range(4):
                 trace[f * ROWS + 36 : f * ROWS + 37, :] = material
-        for side, piece, target, sends, receives in sides:
-            rims[i, piece] = trace[120:160, piece * 128 : piece * 128 + 128]
-
-            @pl.when(sends)
-            def _():
-                halo_copy(i, side, piece, target).start()
-
-        before()
         if first:
             lax.fori_loop(0, 7, build_links, 0)
 
-        for p in range(CHUNKS // 2):
+        for p in range(SPLIT // 2):
             parts = []
             for s in (2 * p, 2 * p + 1):
                 t = s if s < 24 else s + 4
@@ -309,39 +323,71 @@
             place = b + b // 6
             chunk = lax.shift_right_logical(links[place], 7)
             chunk = jnp.where(chunk >= 24, chunk - 4, chunk)
-            result = product(table[...], hot_links[b])
+            result = product(table[0 : SPLIT * ROWS, :], hot_links[b])
+            lanes = jnp.bitwise_and(links[place], 127)
+            total = choose(result, chunk, SPLIT, ROWS)
+            columns = []
+            for q in range(4):
+                part = slice(q * 128, (q + 1) * 128)
+                low = jnp.broadcast_to(lanes[:, part], (8, 128))
+                index = jnp.broadcast_to(chunk[:, part], (8, 128))
+                groups = [total[8 * g : 8 * g + 8, part] for g in range(ROWS // 8)]
+                for s in range(SPLIT, CHUNKS):
+                    t = s if s < 24 else s + 4
+                    mine = index == s
+                    for g in range(ROWS // 8):
+                        source = trace[t // 8 * ROWS + 8 * g : t // 8 * ROWS + 8 * g + 8, t % 8 * 128 : t % 8 * 128 + 128]
+                        groups[g] = jnp.where(mine, jnp.take_along_axis(source, low, axis=1), groups[g])
+                columns.append(jnp.concatenate(groups, axis=0))
             f = place // 2
             half = place - 2 * f
             gathered[
                 pl.ds(pl.multiple_of(f * ROWS, 8), ROWS), pl.ds(pl.multiple_of(half * BLOCK, BLOCK), BLOCK)
-            ] = choose(result, chunk, CHUNKS, ROWS)
+            ] = jnp.concatenate(columns, axis=1)
             return carry
 
-        lax.fori_loop(0, 7, block, 0)
+        lax.fori_loop(0, split, block, 0)
+        middle()
+        if split < 7:
+            lax.fori_loop(split, 7, block, 0)
 
         volume = product(matrix[160:288], stacked[...])
         image[...] = shear * volume[0:64] + lame * volume[64:128]
         solved[...] = solved[...] + now[0:60]
+
+        inner = slice(BLOCK, ELEMS)
+        outer = slice(0, BLOCK)
+        if first:
+            for f in range(3):
+                alpha[f : f + 1, :] = 0.5 * (material + gathered[f * ROWS + 36 : f * ROWS + 37, :])
+            alpha[3:4, inner] = 0.5 * (material[:, inner] + gathered[156:157, inner])
+        for f in range(4):
+            rows = slice(f * ROWS, (f + 1) * ROWS)
+            columns = slice(0, ELEMS) if f < 3 else inner
+            value = alpha[f : f + 1, columns] * (trace[rows, columns] - gathered[rows, columns])
+            flux[rows, columns] = value
+            flux_sum[rows, columns] = flux_sum[rows, columns] + value
+        flux[120:160, outer] = jnp.zeros((ROWS, BLOCK), F32)
+        left = left_over[...] - (image[...] + lifted(flux))[0:60]
+        left_over[...] = left
+        if i < ITERS - 1:
+            field[0:60, :] = scale_old * now[0:60] + scale_new * (left * inverse)
         between()
 
         for side, piece, target, sends, receives in sides:
             @pl.when(receives)
             def _():
                 halo_copy(i, side, piece, target).wait_recv()
-            gathered[120:160, side * 128 : side * 128 + 128] = halo[i, side]
-
+        arrived = jnp.concatenate([halo[i, side] for side in range(4)], axis=1)
         if first:
-            for f in range(4):
-                alpha[f : f + 1, :] = 0.5 * (material + gathered[f * ROWS + 36 : f * ROWS + 37, :])
-        for f in range(4):
-            rows = slice(f * ROWS, (f + 1) * ROWS)
-            value = alpha[f : f + 1, :] * (trace[rows, :] - gathered[rows, :])
-            flux[rows, :] = value
-            flux_sum[rows, :] = flux_sum[rows, :] + value
-        left = left_over[...] - (image[...] + lifted(flux))[0:60]
-        left_over[...] = left
+            alpha[3:4, outer] = 0.5 * (material[:, outer] + arrived[36:37])
+        value = alpha[3:4, outer] * (trace[120:160, outer] - arrived)
+        flux_sum[120:160, outer] = flux_sum[120:160, outer] + value
+        high, low = halves(value)
+        late = (product(rim_lifter, high) + product(rim_rest, high) + product(rim_lifter, low))[0:60]
+        left_over[:, outer] = left_over[:, outer] - late
         if i < ITERS - 1:
-            field[0:60, :] = scale_old * now[0:60] + scale_new * (left * inverse)
+            field[0:60, outer] = field[0:60, outer] - scale_new * (late * inverse[:, outer])
 
     def nothing():
         pass
@@ -387,10 +433,10 @@
         go(*over_second)
 
     pairs = coefficients()
-    step(0, *pairs[0], nothing, ids_middle)
-    step(1, *pairs[1], nothing, answer)
-    step(2, *pairs[2], nothing, nothing)
-    step(3, *pairs[3], params_middle, nothing)
+    step(0, *pairs[0], 4, ids_middle, nothing)
+    step(1, *pairs[1], 7, nothing, answer)
+    step(2, *pairs[2], 7, nothing, nothing)
+    step(3, *pairs[3], 0, params_middle, nothing)
     residual_ref[...] = left_over[...].reshape(60, 1, ELEMS)
     results[0].start()
 
@@ -421,16 +467,8 @@
     lax.fori_loop(0, 8, build_face, 0)
     rate_pack[...] = jnp.zeros_like(rate_pack)
 
-    arrive(*down_second)
-    for j in range(3):
-        params[j * 128 : (j + 1) * 128, :] = jnp.transpose(down_in[pl.ds(j, 128, stride=3), :])
-    arrive(*over_second)
-    for j in range(3):
-        parts = [over_in[pl.ds(a * 3 + j, PD, stride=24), :] for a in range(PA)]
-        params[(3 + j) * 128 : (4 + j) * 128, :] = jnp.transpose(jnp.concatenate(parts, axis=0))
-    for b in range(4):
-        first = [params[(4 * b + j) * 48 : (4 * b + j + 1) * 48, :] for j in range(4)]
-        owned = jnp.concatenate(first, axis=1)
+    def solve(b):
+        owned = jnp.concatenate([params[(4 * b + j) * 48 : (4 * b + j + 1) * 48, :] for j in range(4)], axis=1)
         traction = tractions[b]
         state = owned[12:24]
         strike = owned[24:36] + traction[0:12]
@@ -445,20 +483,32 @@
             inverse_root = lax.rsqrt(square)
             misfit = magnitude - DAMPING * velocity - resist * inverse_sinh(scaled, square * inverse_root)
             velocity = velocity + misfit / (DAMPING + steep * inverse_root)
-        factor = TIME_STEP * velocity / jnp.maximum(magnitude, 1.0)
-        slip = jnp.concatenate([factor * strike, factor * updip], axis=0)
         for j in range(4):
             rank = 4 * b + j
             rate_pack[rank * 16 : rank * 16 + 12, :] = velocity[:, j * 128 : (j + 1) * 128]
+        return velocity, magnitude, strike, updip
+
+    arrive(*down_second)
+    for j in range(3):
+        params[j * 128 : (j + 1) * 128, :] = jnp.transpose(down_in[pl.ds(j, 128, stride=3), :])
+    arrive(*over_second)
+    for j in range(3):
+        parts = [over_in[pl.ds(a * 3 + j, PD, stride=24), :] for a in range(PA)]
+        params[(3 + j) * 128 : (4 + j) * 128, :] = jnp.transpose(jnp.concatenate(parts, axis=0))
+    motion = [solve(b) for b in range(4)]
+    for j in range(2):
+        rate_out[pl.ds(j, 128, stride=2), :] = jnp.transpose(rate_pack[j * 128 : (j + 1) * 128, :])
+    go(*rate_first)
+
+    for b, (velocity, magnitude, strike, updip) in enumerate(motion):
+        factor = TIME_STEP * velocity / jnp.maximum(magnitude, 1.0)
+        slip = jnp.concatenate([factor * strike, factor * updip], axis=0)
         for j in (0, 2):
             parts = [slip[:, j * 128 : (j + 1) * 128], slip[:, (j + 1) * 128 : (j + 2) * 128]]
             high, low = halves(jnp.concatenate(parts, axis=0))
             at = (4 * b + j) * 24
             table_back[at : at + 48, 0:128] = high
             table_back[at : at + 48, 128:256] = low
-    for j in range(2):
-        rate_out[pl.ds(j, 128, stride=2), :] = jnp.transpose(rate_pack[j * 128 : (j + 1) * 128, :])
-    go(*rate_first)
 
     flux[...] = jnp.zeros_like(flux)
 

time: 47.9 us -> 47.1 us (0.983)
  Pallas kernels: 46.5 us -> 45.7 us
    pallas_call x1, Pallas kernels: 44.7 us -> 43.9 us  [on_device(): pl.pallas_call(kernel, out_shape=(jax.ShapeDtypeStruct((60, 1, ELEMS), F3...]
where the time goes in v5:
time: 47.1 us; the launch traced here: 47 us
  Pallas kernels  45.7 us (97%)
  between operations  1.29 us (3%)
    pallas_call x1, Pallas kernels, on_device(): pl.pallas_call(kernel, out_shape=(jax.ShapeDtypeStruct((60, 1, ELEMS), F3...  43.9 us
    pallas_call x1, Pallas kernels, on_device(): pl.pallas_call(hand_over, out_shape=(jax.ShapeDtypeStruct((480, 128), F32...  1.81 us

profile of v5, /device:TPU:1, one launch (start us, length us, event | category | flops | bytes accessed | tf_op | source)
XLA Modules:
  0.0 47.0 jit_solution(7310421979720935512)
XLA Ops:
  1.3 43.9 %window.1 = (f32[60,1,1024]{2,1,0:T(1,128)}, f32[60,1,1024]{2,1,0:T(1,128)}, f32[12,512]{1,0:T(8,128)}) custom-call(s32[1,1]{1,0:T(1,128)S(6)} %copy.22.count_ref, f32[60,1,1024]{2,1,0:T(1,128)} %bitcast.12, f32[1,1024]{1,0:T(1,128)} %bitcast.20, f32[1,1024]{1,0:T(1,128)} %bitcast.21, f32[60,60]{1,0:T(8,128)} %stiff_shear_hbm.1, f32[60,60]{1,0:T(8,128)} %stiff_lame_hbm.1, ...), custom_call_target="tpu_custom_call" | custom-call | tf_op jit(solution)/shard_map/window/pallas_call | solution.py:661
  45.2 1.8 %hand_over.1 = (f32[480,128]{1,0:T(8,128)}, f32[480,128]{1,0:T(8,128)}, f32[12,512]{1,0:T(8,128)}) custom-call(f32[480,128]{1,0:T(8,128)} %bitcast.13, f32[480,128]{1,0:T(8,128)} %bitcast.14, f32[12,512]{1,0:T(8,128)} %get-tuple-element.11.rate_ref), custom_call_target="tpu_custom_call" | custom-call | tf_op jit(solution)/shard_map/hand_over/pallas_call | solution.py:690

commit v6 on v5

--- a/solution.py
+++ b/solution.py
@@ -28,6 +28,9 @@
 BLOCK = 512
 CHUNKS = 28
 SPLIT = 18
+SEND_SPLIT = 20
+FAR_ROW = (4, 3, 5, 2, 6, 1, 7)
+FAR_COLUMN = (6, 10, 7, 9, 2, 14, 5, 11, 8, 3, 13, 1, 15, 4, 12)
 RANKS = 16
 
 
@@ -63,6 +66,24 @@
         part = result[s * rows : (s + 1) * rows].reshape(rows // 8, 8, width)
         total = jnp.where((index == s)[None], part, total)
     return total.reshape(rows, width)
+
+
+def lane_gather(total, rows_ref, chunk, lanes, chunks, rows):
+    columns = []
+    for q in range(4):
+        part = slice(q * 128, (q + 1) * 128)
+        low = jnp.broadcast_to(lanes[:, part], (8, 128))
+        index = jnp.broadcast_to(chunk[:, part], (8, 128))
+        groups = [total[8 * g : 8 * g + 8, part] for g in range(rows // 8)]
+        for s in chunks:
+            t = s if len(chunks) + chunks[0] == 32 or s < 24 else s + 4
+            mine = index == s
+            for g in range(rows // 8):
+                at = t // 8 * ROWS + 8 * g
+                source = rows_ref[at : at + 8, t % 8 * 128 : t % 8 * 128 + 128]
+                groups[g] = jnp.where(mine, jnp.take_along_axis(source, low, axis=1), groups[g])
+        columns.append(jnp.concatenate(groups, axis=0))
+    return jnp.concatenate(columns, axis=1)
 
 
 def inverse_sinh(size, root):
@@ -141,8 +162,8 @@
         )
 
     def go(kind, source, landing, size, sems):
-        mine, peers = (along, PA) if kind is row_copy else (depth, PD)
-        for i in range(1, peers):
+        mine, order = (along, FAR_ROW) if kind is row_copy else (depth, FAR_COLUMN)
+        for i in order:
             kind(i, source, landing, size, sems, True).start()
         own = pl.ds(pl.multiple_of(mine * size, 8), size)
         landing[own, :] = source[own, :]
@@ -326,24 +347,12 @@
             result = product(table[0 : SPLIT * ROWS, :], hot_links[b])
             lanes = jnp.bitwise_and(links[place], 127)
             total = choose(result, chunk, SPLIT, ROWS)
-            columns = []
-            for q in range(4):
-                part = slice(q * 128, (q + 1) * 128)
-                low = jnp.broadcast_to(lanes[:, part], (8, 128))
-                index = jnp.broadcast_to(chunk[:, part], (8, 128))
-                groups = [total[8 * g : 8 * g + 8, part] for g in range(ROWS // 8)]
-                for s in range(SPLIT, CHUNKS):
-                    t = s if s < 24 else s + 4
-                    mine = index == s
-                    for g in range(ROWS // 8):
-                        source = trace[t // 8 * ROWS + 8 * g : t // 8 * ROWS + 8 * g + 8, t % 8 * 128 : t % 8 * 128 + 128]
-                        groups[g] = jnp.where(mine, jnp.take_along_axis(source, low, axis=1), groups[g])
-                columns.append(jnp.concatenate(groups, axis=0))
+            total = lane_gather(total, trace, chunk, lanes, range(SPLIT, CHUNKS), ROWS)
             f = place // 2
             half = place - 2 * f
             gathered[
                 pl.ds(pl.multiple_of(f * ROWS, 8), ROWS), pl.ds(pl.multiple_of(half * BLOCK, BLOCK), BLOCK)
-            ] = jnp.concatenate(columns, axis=1)
+            ] = total
             return carry
 
         lax.fori_loop(0, split, block, 0)
@@ -440,7 +449,7 @@
     residual_ref[...] = left_over[...].reshape(60, 1, ELEMS)
     results[0].start()
 
-    for p in range(16):
+    for p in range(SEND_SPLIT // 2):
         parts = []
         for s in (2 * p, 2 * p + 1):
             f, j = s // 8, s % 8
@@ -454,8 +463,10 @@
         hot = onehot(low.astype(jnp.int32), 128, BLOCK).astype(BF16)
         hot_send[0:128, :] = hot
         hot_send[128:256, :] = hot
-        result = product(table_send[...], hot_send[...])
-        tractions[b] = choose(result, high.astype(jnp.int32), 32, ROWS)
+        result = product(table_send[0 : SEND_SPLIT * ROWS, :], hot_send[...])
+        chunk = high.astype(jnp.int32)
+        total = choose(result, chunk, SEND_SPLIT, ROWS)
+        tractions[b] = lane_gather(total, flux_sum, chunk, low.astype(jnp.int32), range(SEND_SPLIT, 32), ROWS)
 
     def build_face(b, carry):
         low = jnp.concatenate([face_maps[pl.ds(32 + 4 * b + j, 1), :] for j in range(4)], axis=1)

time: 47.1 us -> 46.5 us (0.987)
  Pallas kernels: 45.7 us -> 45.1 us
    pallas_call x1, Pallas kernels: 43.9 us -> 43.3 us  [on_device(): pl.pallas_call(kernel, out_shape=(jax.ShapeDtypeStruct((60, 1, ELEMS), F3...]
where the time goes in v6:
time: 46.5 us; the launch traced here: 46.4 us
  Pallas kernels  45.1 us (97%)
  between operations  1.29 us (3%)
    pallas_call x1, Pallas kernels, on_device(): pl.pallas_call(kernel, out_shape=(jax.ShapeDtypeStruct((60, 1, ELEMS), F3...  43.3 us
    pallas_call x1, Pallas kernels, on_device(): pl.pallas_call(hand_over, out_shape=(jax.ShapeDtypeStruct((480, 128), F32...  1.81 us

profile of v6, /device:TPU:1, one launch (start us, length us, event | category | flops | bytes accessed | tf_op | source)
XLA Modules:
  0.0 46.4 jit_solution(5140338223414882971)
XLA Ops:
  1.3 43.3 %window.1 = (f32[60,1,1024]{2,1,0:T(1,128)}, f32[60,1,1024]{2,1,0:T(1,128)}, f32[12,512]{1,0:T(8,128)}) custom-call(s32[1,1]{1,0:T(1,128)S(6)} %copy.22.count_ref, f32[60,1,1024]{2,1,0:T(1,128)} %bitcast.12, f32[1,1024]{1,0:T(1,128)} %bitcast.20, f32[1,1024]{1,0:T(1,128)} %bitcast.21, f32[60,60]{1,0:T(8,128)} %stiff_shear_hbm.1, f32[60,60]{1,0:T(8,128)} %stiff_lame_hbm.1, ...), custom_call_target="tpu_custom_call" | custom-call | tf_op jit(solution)/shard_map/window/pallas_call | solution.py:672
  44.6 1.8 %hand_over.1 = (f32[480,128]{1,0:T(8,128)}, f32[480,128]{1,0:T(8,128)}, f32[12,512]{1,0:T(8,128)}) custom-call(f32[480,128]{1,0:T(8,128)} %bitcast.13, f32[480,128]{1,0:T(8,128)} %bitcast.14, f32[12,512]{1,0:T(8,128)} %get-tuple-element.11.rate_ref), custom_call_target="tpu_custom_call" | custom-call | tf_op jit(solution)/shard_map/hand_over/pallas_call | solution.py:701

commit v7 on v6

--- a/solution.py
+++ b/solution.py
@@ -129,9 +129,9 @@
     ]
 
     barrier = pltpu.get_barrier_semaphore()
-    for i in range(1, PA):
+    for i in FAR_ROW:
         pl.semaphore_signal(barrier, inc=1, device_id=(lax.rem(along + i, PA), depth), device_id_type=MESH)
-    for i in range(1, PD):
+    for i in FAR_COLUMN:
         pl.semaphore_signal(barrier, inc=1, device_id=(along, lax.rem(depth + i, PD)), device_id_type=MESH)
 
     for fetch in fetches[3:]:
@@ -468,14 +468,6 @@
         total = choose(result, chunk, SEND_SPLIT, ROWS)
         tractions[b] = lane_gather(total, flux_sum, chunk, low.astype(jnp.int32), range(SEND_SPLIT, 32), ROWS)
 
-    def build_face(b, carry):
-        low = jnp.concatenate([face_maps[pl.ds(32 + 4 * b + j, 1), :] for j in range(4)], axis=1)
-        hot = onehot(low.astype(jnp.int32), 128, BLOCK).astype(BF16)
-        hot_face[b, 0:128, :] = hot
-        hot_face[b, 128:256, :] = hot
-        return carry
-
-    lax.fori_loop(0, 8, build_face, 0)
     rate_pack[...] = jnp.zeros_like(rate_pack)
 
     def solve(b):
@@ -521,6 +513,14 @@
             table_back[at : at + 48, 0:128] = high
             table_back[at : at + 48, 128:256] = low
 
+    def build_face(b, carry):
+        low = jnp.concatenate([face_maps[pl.ds(32 + 4 * b + j, 1), :] for j in range(4)], axis=1)
+        hot = onehot(low.astype(jnp.int32), 128, BLOCK).astype(BF16)
+        hot_face[b, 0:128, :] = hot
+        hot_face[b, 128:256, :] = hot
+        return carry
+
+    lax.fori_loop(0, 8, build_face, 0)
     flux[...] = jnp.zeros_like(flux)
 
     def place_back(b, carry):

time: 46.5 us -> 46.3 us (level)
  no operation moved by 1% of the time
where the time goes in v7:
time: 46.3 us; the launch traced here: 46.1 us
  Pallas kernels  44.8 us (97%)
  between operations  1.29 us (3%)
    pallas_call x1, Pallas kernels, on_device(): pl.pallas_call(kernel, out_shape=(jax.ShapeDtypeStruct((60, 1, ELEMS), F3...  43 us
    pallas_call x1, Pallas kernels, on_device(): pl.pallas_call(hand_over, out_shape=(jax.ShapeDtypeStruct((480, 128), F32...  1.81 us

profile of v7, /device:TPU:1, one launch (start us, length us, event | category | flops | bytes accessed | tf_op | source)
XLA Modules:
  0.0 46.1 jit_solution(10097789257540669372)
XLA Ops:
  1.3 43.0 %window.1 = (f32[60,1,1024]{2,1,0:T(1,128)}, f32[60,1,1024]{2,1,0:T(1,128)}, f32[12,512]{1,0:T(8,128)}) custom-call(s32[1,1]{1,0:T(1,128)S(6)} %copy.22.count_ref, f32[60,1,1024]{2,1,0:T(1,128)} %bitcast.12, f32[1,1024]{1,0:T(1,128)} %bitcast.20, f32[1,1024]{1,0:T(1,128)} %bitcast.21, f32[60,60]{1,0:T(8,128)} %stiff_shear_hbm.1, f32[60,60]{1,0:T(8,128)} %stiff_lame_hbm.1, ...), custom_call_target="tpu_custom_call" | custom-call | tf_op jit(solution)/shard_map/window/pallas_call | solution.py:672
  44.3 1.8 %hand_over.1 = (f32[480,128]{1,0:T(8,128)}, f32[480,128]{1,0:T(8,128)}, f32[12,512]{1,0:T(8,128)}) custom-call(f32[480,128]{1,0:T(8,128)} %bitcast.13, f32[480,128]{1,0:T(8,128)} %bitcast.14, f32[12,512]{1,0:T(8,128)} %get-tuple-element.11.rate_ref), custom_call_target="tpu_custom_call" | custom-call | tf_op jit(solution)/shard_map/hand_over/pallas_call | solution.py:701

commit v8 on v7

--- a/solution.py
+++ b/solution.py
@@ -27,7 +27,7 @@
 ROWS = 40
 BLOCK = 512
 CHUNKS = 28
-SPLIT = 18
+SPLIT = 16
 SEND_SPLIT = 20
 FAR_ROW = (4, 3, 5, 2, 6, 1, 7)
 FAR_COLUMN = (6, 10, 7, 9, 2, 14, 5, 11, 8, 3, 13, 1, 15, 4, 12)

time: 46.3 us -> 46.2 us (level)
  no operation moved by 1% of the time
where the time goes in v8:
time: 46.2 us; the launch traced here: 46.1 us
  Pallas kernels  44.8 us (97%)
  between operations  1.29 us (3%)
    pallas_call x1, Pallas kernels, on_device(): pl.pallas_call(kernel, out_shape=(jax.ShapeDtypeStruct((60, 1, ELEMS), F3...  43 us
    pallas_call x1, Pallas kernels, on_device(): pl.pallas_call(hand_over, out_shape=(jax.ShapeDtypeStruct((480, 128), F32...  1.81 us

profile of v8, /device:TPU:1, one launch (start us, length us, event | category | flops | bytes accessed | tf_op | source)
XLA Modules:
  0.0 46.1 jit_solution(833933584420615662)
XLA Ops:
  1.3 43.0 %window.1 = (f32[60,1,1024]{2,1,0:T(1,128)}, f32[60,1,1024]{2,1,0:T(1,128)}, f32[12,512]{1,0:T(8,128)}) custom-call(s32[1,1]{1,0:T(1,128)S(6)} %copy.22.count_ref, f32[60,1,1024]{2,1,0:T(1,128)} %bitcast.12, f32[1,1024]{1,0:T(1,128)} %bitcast.20, f32[1,1024]{1,0:T(1,128)} %bitcast.21, f32[60,60]{1,0:T(8,128)} %stiff_shear_hbm.1, f32[60,60]{1,0:T(8,128)} %stiff_lame_hbm.1, ...), custom_call_target="tpu_custom_call" | custom-call | tf_op jit(solution)/shard_map/window/pallas_call | solution.py:672
  44.3 1.8 %hand_over.1 = (f32[480,128]{1,0:T(8,128)}, f32[480,128]{1,0:T(8,128)}, f32[12,512]{1,0:T(8,128)}) custom-call(f32[480,128]{1,0:T(8,128)} %bitcast.13, f32[480,128]{1,0:T(8,128)} %bitcast.14, f32[12,512]{1,0:T(8,128)} %get-tuple-element.11.rate_ref), custom_call_target="tpu_custom_call" | custom-call | tf_op jit(solution)/shard_map/hand_over/pallas_call | solution.py:701
